TPU v7x, 32 devices: a whole 2x2x4 slice. The times are simulated.
32 devices in a mesh: seq: 8 (over z, y), head: 4 (over x, core).
Axes of the slice: x: 2, y: 2, z: 4, core: 2. Of those that a mesh axis runs over, the one named last changes fastest.
Arguments:
- queries: bfloat16 [1024, 4096], P('seq', 'head'), may hold values from -6 to 6
- keys: bfloat16 [1024, 4096], P('seq', 'head'), may hold values from -6 to 6
- values: bfloat16 [1024, 4096], P('seq', 'head'), may hold values from -6 to 6
- hidden: bfloat16 [1024, 2048], P('seq', 'head'), may hold values from -6 to 6
- gate_weight: bfloat16 [2048, 128], P('head'), may hold values from -0.125 to 0.125
- level_slot: int32 [4], replicated, may hold values from 0 to 3, each once
- out_grad: bfloat16 [1024, 4096], P('seq', 'head'), may hold values from -6 to 6
Outputs:
- mixed: bfloat16 [1024, 4096], P('seq', 'head')
- grad_queries: bfloat16 [1024, 4096], P('seq', 'head')
- grad_keys: bfloat16 [1024, 4096], P('seq', 'head')
- grad_values: bfloat16 [1024, 4096], P('seq', 'head')
- grad_hidden: bfloat16 [1024, 2048], P('seq', 'head')
Inputs may be any that keep to these rules, and one draw needn't show every extreme that they name: `level_slot`: each column index of a head's block appears once.
All inputs are finite; a program needn't handle non-finite values.
Results may differ from a plain program's by a relative error of at most 0.01.
Values may be sent and summed in bfloat16 or wider, within the bound.
A program may use at most 64 MiB of HBM per device.

v0:
```python
import jax
import jax.numpy as jnp
from jax import lax
from jax.sharding import PartitionSpec as P

DK = 128
SPAN = 128


HIGH = lax.Precision.HIGHEST


def from_partner(block, axis, stride):
    count = lax.axis_size(axis)
    route = []
    for low in range(count):
        high = low | 1 << stride
        if high != low and high < count:
            route += [(low, high), (high, low)]
    return lax.ppermute(block, axis, route)


def local(queries, keys, values, hidden, gate_weight, level_slot, out_grad):
    tok_rows = queries.shape[0]
    heads_here = queries.shape[1] // DK
    levels = level_slot.shape[0]
    rows_here = heads_here * levels
    span_count = tok_rows // SPAN
    local_bits = span_count.bit_length() - 1
    device_bits = lax.axis_size("seq").bit_length() - 1
    seq_index = lax.axis_index("seq")
    columns = gate_weight
    logits = lax.psum_scatter(
        lax.dot_general(
            columns, hidden, (((0,), (1,)), ((), ())), preferred_element_type=jnp.float32
        ),
        "head",
        scatter_dimension=0,
        tiled=True,
    )
    slot_table = (level_slot[:, None] == jnp.arange(levels, dtype=jnp.int32)[None, :]).astype(
        jnp.float32
    )
    chosen = jnp.einsum(
        "lm,hmt->hlt", slot_table, logits.reshape(heads_here, levels, tok_rows), precision=HIGH
    )
    weights = jnp.transpose(jax.nn.softplus(chosen), (2, 0, 1))
    query_heads = queries.reshape(tok_rows, heads_here, DK)
    grad_heads = out_grad.reshape(tok_rows, heads_here, DK)
    query_blocks = queries.reshape(span_count, SPAN, heads_here, DK)
    key_blocks = keys.reshape(span_count, SPAN, heads_here, DK)
    value_blocks = values.reshape(span_count, SPAN, heads_here, DK)
    position = jnp.arange(SPAN)
    causal = (position[:, None] >= position[None, :]).astype(jnp.float32)
    scores = jnp.einsum(
        "nchd,nshd->nhcs", query_blocks, key_blocks, preferred_element_type=jnp.float32
    )
    attend = (scores * causal / SPAN).astype(jnp.bfloat16)
    intra = jnp.einsum(
        "nhcs,nshe->nche", attend, value_blocks, preferred_element_type=jnp.float32
    ).reshape(tok_rows, heads_here, DK)
    weighted = (weights[..., None] * grad_heads[:, :, None, :]).astype(jnp.bfloat16)
    device_grads = jnp.einsum(
        "thd,thje->hjde",
        query_heads,
        weighted[:, :, 1 + local_bits :],
        preferred_element_type=jnp.float32,
    )
    span_states = jnp.einsum(
        "nchd,nche->nhde", key_blocks, value_blocks, preferred_element_type=jnp.float32
    )
    device_state = span_states.sum(0)
    group = device_state
    lower_states = []
    for bit_pos in range(device_bits):
        partner = from_partner(group.astype(jnp.bfloat16), "seq", bit_pos).astype(group.dtype)
        upper_half = seq_index >> bit_pos & 1
        lower_states.append(
            jnp.where(upper_half == 1, partner, 0.0) / float((1 << bit_pos) * tok_rows)
        )
        group = group + partner
    pending = device_grads
    carried = jnp.zeros_like(device_state)
    for bit_pos in range(device_bits):
        partner_pending = from_partner(pending.astype(jnp.bfloat16), "seq", bit_pos).astype(
            pending.dtype
        )
        upper_half = seq_index >> bit_pos & 1
        scale_here = float((1 << bit_pos) * tok_rows)
        carried = carried + jnp.where(upper_half == 0, partner_pending[:, 0], 0.0) / scale_here
        pending = pending[:, 1:] + partner_pending[:, 1:]
    device_level = jnp.stack(lower_states, 1).astype(jnp.bfloat16)
    device_outs = jnp.einsum(
        "thd,hjde->tjhe", query_heads, device_level, preferred_element_type=jnp.float32
    )
    mixed = weights[:, :, 0:1] * intra + jnp.einsum(
        "thj,tjhe->the", weights[:, :, 1:], device_outs, precision=HIGH
    )
    first_grad = jnp.sum(grad_heads * intra, -1)
    later_grad = jnp.einsum(
        "the,tjhe->thj", grad_heads.astype(jnp.float32), device_outs, precision=HIGH
    )
    weight_grad = jnp.concatenate([first_grad[:, :, None], later_grad], 2)
    first_blocks = weighted[:, :, 0].reshape(span_count, SPAN, heads_here, DK)
    grad_score = (
        jnp.einsum(
            "nche,nshe->nhcs", first_blocks, value_blocks, preferred_element_type=jnp.float32
        )
        * causal
        / SPAN
    ).astype(jnp.bfloat16)
    grad_query = jnp.einsum(
        "nhcs,nshd->nchd", grad_score, key_blocks, preferred_element_type=jnp.float32
    ).reshape(tok_rows, heads_here, DK)
    grad_key = jnp.einsum(
        "nhcs,nchd->nshd", grad_score, query_blocks, preferred_element_type=jnp.float32
    ).reshape(tok_rows, heads_here, DK)
    grad_value = jnp.einsum(
        "nhcs,nche->nshe", attend, first_blocks, preferred_element_type=jnp.float32
    ).reshape(tok_rows, heads_here, DK)
    device_back = jnp.einsum(
        "the,hjde->tjhd", grad_heads, device_level, preferred_element_type=jnp.float32
    )
    grad_query = grad_query + jnp.einsum(
        "thj,tjhd->thd", weights[:, :, 1 + local_bits :], device_back, precision=HIGH
    )
    state_total = carried[None].astype(jnp.bfloat16)
    grad_key = grad_key + jnp.einsum(
        "nche,nhde->nchd", value_blocks, state_total, preferred_element_type=jnp.float32
    ).reshape(tok_rows, heads_here, DK)
    grad_value = grad_value + jnp.einsum(
        "nchd,nhde->nche", key_blocks, state_total, preferred_element_type=jnp.float32
    ).reshape(tok_rows, heads_here, DK)
    chosen_grad = jnp.transpose(weight_grad, (1, 2, 0)) * jax.nn.sigmoid(chosen)
    logit_grad = (
        jnp.einsum("lm,hlt->hmt", slot_table, chosen_grad, precision=HIGH)
        .reshape(rows_here, tok_rows)
        .astype(jnp.bfloat16)
    )
    columns = gate_weight
    grad_hidden = lax.dot_general(
        lax.all_gather(logit_grad, "head", axis=0, tiled=True),
        columns,
        (((0,), (1,)), ((), ())),
        preferred_element_type=jnp.float32,
    )
    width_all = heads_here * DK
    return (
        mixed.reshape(tok_rows, width_all).astype(jnp.bfloat16),
        grad_query.reshape(tok_rows, width_all).astype(jnp.bfloat16),
        grad_key.reshape(tok_rows, width_all).astype(jnp.bfloat16),
        grad_value.reshape(tok_rows, width_all).astype(jnp.bfloat16),
        grad_hidden.astype(jnp.bfloat16),
    )


def solution(mesh):
    placed = (
        P("seq", "head"),
        P("seq", "head"),
        P("seq", "head"),
        P("seq", "head"),
        P("head", None),
        P(),
        P("seq", "head"),
    )
    return jax.shard_map(
        local,
        mesh=mesh,
        in_specs=placed,
        out_specs=(
            P("seq", "head"),
            P("seq", "head"),
            P("seq", "head"),
            P("seq", "head"),
            P("seq", "head"),
        ),
        check_vma=False,
    )
```

profile of v0, /device:TPU:0, one launch (start us, length us, event | category | flops | bytes accessed | tf_op | source)
XLA Modules:
  0.0 101.2 jit_solution(2674402185200336692)
XLA Ops:
  7.2 1.9 %fusion.76 = f32[128,128]{1,0:T(8,128)} fusion(bf16[512,128]{1,0:T(8,128)(2,1)} %param.11, bf16[128,512]{1,0:T(8,128)(2,1)} %param.10), kind=kOutput, calls=%fused_computation.106 | convolution fusion | flops 16777216 | bytes 327680 | tf_op jit(solution)/shard_map/dot_general | solution.py:34
  9.1 1.0 %copy.75 = bf16[16,8,8,128]{3,2,1,0:T(8,128)(2,1)S(1)} copy(bf16[16,8,8,128]{3,1,2,0:T(8,128)(2,1)} %bitcast.177) | data formatting | bytes 524288
  10.4 0.9 fusion.74
  11.3 3.0 %collective-permute-start = (bf16[8,128,128]{2,1,0:T(8,128)(2,1)}, bf16[8,128,128]{2,1,0:T(8,128)(2,1)}, u32[]{:S(2)}, u32[]{:S(2)}) collective-permute-start(bf16[8,128,128]{2,1,0:T(8,128)(2,1)} %get-tuple-element.17), channel_id=1, source_target_pairs={{0,4},{4,0},{8,12},{12,8},{16,20},{20,16},{24,28},{28,24},{1,5},{5... | collective-permute-start | bytes 786440 | tf_op jit(solution)/shard_map/ppermute | solution.py:20
  14.9 1.0 copy.22
  15.9 1.0 %fusion.7 = bf16[8,128,128]{2,1,0:T(8,128)(2,1)} fusion(bf16[128,8,128]{0,2,1:T(8,128)(2,1)S(1)} %copy.25, f32[128,128]{1,0:T(8,128)S(1)} %fusion.50, bf16[128,1024]{1,0:T(8,128)(2,1)S(1)} %copy-done.1), kind=kOutput, calls=%fused_computation.18 | convolution fusion | flops 33947648 | bytes 851968 | tf_op jit(solution)/shard_map/nchd,nshd->nhcs/dot_general | solution.py:55
  16.9 16.3 %reduce-scatter.2.cloned.1.call-done = f32[32,128]{1,0:T(8,128)} async-done(((f32[128,128]{1,0:T(8,128)}), f32[32,128]{1,0:T(8,128)}) %reduce-scatter.2.cloned.1.call-update) | async-done | bytes 16400 | tf_op jit(solution)/shard_map/reduce_scatter | solution.py:33
  33.2 1.0 compare_select_fusion
  34.2 1.7 %multiply_convert_fusion = bf16[128,8,4,128]{3,0,1,2:T(8,128)(2,1)S(1)} fusion(f32[128,8,128]{2,0,1:T(8,128)} %copy.22, f32[128,8,4]{0,1,2:T(8,128)S(1)} %copy.20), kind=kLoop, calls=%fused_computation | loop fusion | flops 1048576 | bytes 1589248 | tf_op jit(solution)/shard_map/convert_element_type | solution.py:62
  35.9 1.0 fusion.27
  36.9 1.5 %collective-permute-start.1 = (bf16[8,128,128]{2,1,0:T(8,128)(2,1)S(1)}, bf16[8,128,128]{2,1,0:T(8,128)(2,1)S(1)}, u32[]{:S(2)}, u32[]{:S(2)}) collective-permute-start(bf16[8,128,128]{2,1,0:T(8,128)(2,1)S(1)} %fusion.27), channel_id=1, source_target_pairs={{0,8},{8,0},{4,12},{12,4},{16,24},{24,16},{20,28},{28,20},{1,9},{9... | collective-permute-start | bytes 786440 | tf_op jit(solution)/shard_map/ppermute | solution.py:20
  38.9 5.6 %collective-permute-done.1 = bf16[8,128,128]{2,1,0:T(8,128)(2,1)S(1)} collective-permute-done((bf16[8,128,128]{2,1,0:T(8,128)(2,1)S(1)}, bf16[8,128,128]{2,1,0:T(8,128)(2,1)S(1)}, u32[]{:S(2)}, u32[]{:S(2)}) %collective-permute-start.1) | collective-permute-done | bytes 262176 | tf_op jit(solution)/shard_map/ppermute | solution.py:20
  44.5 1.2 %fusion.30 = (bf16[8,1,128,128]{3,2,0,1:T(8,128)(2,1)S(1)}, bf16[8,128,128]{2,1,0:T(8,128)(2,1)S(1)}, bf16[8,1,128,128]{3,2,0,1:T(8,128)(2,1)S(1)}) fusion(bf16[8,128,128]{2,1,0:T(8,128)(2,1)} %collective-permute-done, pred[]{:T(512)S(6)} %eq.34, bf16[8,128,128]{2,1,0:T(8,128)(2,1)S(1)} %collective-permute-done.1, f32[8,128,128]{2,1,0:T(8,128)S(1)} %get-tuple-element.18, ...), kind=kLoop, calls=%fused_computation.55 | loop fusion | flops 1441792 | bytes 1835010 | tf_op jit(solution)/shard_map/stack | solution.py:92
  45.7 2.5 %collective-permute-start.2 = (bf16[8,128,128]{2,1,0:T(8,128)(2,1)S(1)}, bf16[8,128,128]{2,1,0:T(8,128)(2,1)S(1)}, u32[]{:S(2)}, u32[]{:S(2)}) collective-permute-start(bf16[8,128,128]{2,1,0:T(8,128)(2,1)S(1)} %get-tuple-element.15), channel_id=1, source_target_pairs={{0,16},{16,0},{4,20},{20,4},{8,24},{24,8},{12,28},{28,12},{1,17},{... | collective-permute-start | bytes 786440 | tf_op jit(solution)/shard_map/ppermute | solution.py:20
  48.2 1.1 %fusion.41 = f32[8,128,128]{2,1,0:T(8,128)} fusion(bf16[8,128,128]{2,1,0:T(8,128)(2,1)S(1)} %copy-done.2, bf16[128,8,4,128]{3,0,1,2:T(8,128)(2,1)S(1)} %multiply_convert_fusion), kind=kOutput, calls=%fused_computation.67 | convolution fusion | flops 33554432 | bytes 1048576 | tf_op jit(solution)/shard_map/nhcs,nche->nshe/dot_general | solution.py:118
  49.3 1.5 %collective-permute-start.3 = (bf16[8,3,128,128]{2,3,1,0:T(8,128)(2,1)S(1)}, bf16[8,3,128,128]{2,3,1,0:T(8,128)(2,1)S(1)}, u32[]{:S(2)}, u32[]{:S(2)}) collective-permute-start(bf16[8,3,128,128]{2,3,1,0:T(8,128)(2,1)S(1)} %get-tuple-element.23), channel_id=1, source_target_pairs={{0,4},{4,0},{8,12},{12,8},{16,20},{20,16},{24,28},{28,24},{1,5},{5... | collective-permute-start | bytes 2359304 | tf_op jit(solution)/shard_map/ppermute | solution.py:20
  51.1 7.9 %collective-permute-done.2 = bf16[8,128,128]{2,1,0:T(8,128)(2,1)S(1)} collective-permute-done((bf16[8,128,128]{2,1,0:T(8,128)(2,1)S(1)}, bf16[8,128,128]{2,1,0:T(8,128)(2,1)S(1)}, u32[]{:S(2)}, u32[]{:S(2)}) %collective-permute-start.2) | collective-permute-done | bytes 262176 | tf_op jit(solution)/shard_map/ppermute | solution.py:20
  59.8 7.0 %collective-permute-done.3 = bf16[8,3,128,128]{2,3,1,0:T(8,128)(2,1)S(1)} collective-permute-done((bf16[8,3,128,128]{2,3,1,0:T(8,128)(2,1)S(1)}, bf16[8,3,128,128]{2,3,1,0:T(8,128)(2,1)S(1)}, u32[]{:S(2)}, u32[]{:S(2)}) %collective-permute-start.3) | collective-permute-done | bytes 786464 | tf_op jit(solution)/shard_map/ppermute | solution.py:20
  67.2 1.5 %collective-permute-start.4 = (bf16[8,2,128,128]{2,3,1,0:T(8,128)(2,1)S(1)}, bf16[8,2,128,128]{2,3,1,0:T(8,128)(2,1)S(1)}, u32[]{:S(2)}, u32[]{:S(2)}) collective-permute-start(bf16[8,2,128,128]{2,3,1,0:T(8,128)(2,1)S(1)} %get-tuple-element.10), channel_id=1, source_target_pairs={{0,8},{8,0},{4,12},{12,4},{16,24},{24,16},{20,28},{28,20},{1,9},{9... | collective-permute-start | bytes 1572872 | tf_op jit(solution)/shard_map/ppermute | solution.py:20
  68.9 1.0 %fusion.11 = bf16[128,8,128]{0,2,1:T(8,128)(2,1)} fusion(f32[128,8,128]{0,2,1:T(8,128)S(1)} %fusion.1, bf16[8,128,128]{2,1,0:T(8,128)(2,1)S(1)} %fusion.8, bf16[128,8,128]{0,2,1:T(8,128)(2,1)S(1)} %copy.16), kind=kOutput, calls=%fused_computation.22 | convolution fusion | flops 33816576 | bytes 1310720 | tf_op jit(solution)/shard_map/nhcs,nshd->nchd/dot_general | solution.py:112
  69.9 1.0 %multiply_reduce_fusion = (f32[128,8]{0,1:T(8,128)S(1)}, bf16[128,8,128]{0,2,1:T(8,128)(2,1)}) fusion(bf16[128,1024]{0,1:T(8,128)(2,1)S(1)} %copy.21, f32[128,8,128]{0,2,1:T(8,128)S(1)} %get-tuple-element.21, f32[128,8]{0,1:T(8,128)S(1)} %bitcast.188, bf16[8,128,128]{2,1,0:T(8,128)(2,1)S(1)} %copy-done.2, bf16[128,1024]{1,0:T(8,128)(2,1)S(1)} %copy-done), kind=kOutput, calls=%fused_computation.49 | convolution fusion | flops 34339840 | bytes 1581056 | tf_op jit(solution)/shard_map/nhcs,nshe->nche/dot_general | solution.py:59
  71.0 7.4 %collective-permute-done.4 = bf16[8,2,128,128]{2,3,1,0:T(8,128)(2,1)S(1)} collective-permute-done((bf16[8,2,128,128]{2,3,1,0:T(8,128)(2,1)S(1)}, bf16[8,2,128,128]{2,3,1,0:T(8,128)(2,1)S(1)}, u32[]{:S(2)}, u32[]{:S(2)}) %collective-permute-start.4) | collective-permute-done | bytes 524320 | tf_op jit(solution)/shard_map/ppermute | solution.py:20
  78.5 0.8 fusion.21
  79.2 0.5 collective-permute-start.5
  79.9 1.8 %copy.33 = bf16[128,1024]{1,0:T(8,128)(2,1)} copy(bf16[128,1024]{0,1:T(8,128)(2,1)} %bitcast.182) | data formatting | bytes 524288
  81.7 1.8 %copy.32 = bf16[128,1024]{1,0:T(8,128)(2,1)} copy(bf16[128,1024]{0,1:T(8,128)(2,1)} %bitcast.186) | data formatting | bytes 524288
  83.5 5.3 %all_gather.3 = bf16[128,128]{1,0:T(8,128)(2,1)S(1)} all-gather(bf16[32,128]{1,0:T(8,128)(2,1)S(1)} %bitcast.189), channel_id=1, replica_groups=mesh['seq'=8,'head'=4] {'head'}, dimensions={0}, use_global_device_ids=true | all-gather | bytes 40960 | tf_op jit(solution)/shard_map/all_gather | solution.py:142
  88.8 0.9 convolution_convert_fusion
  89.7 0.9 collective-permute-done.5
  90.6 1.1 %fusion.25 = bf16[8,1,128,128]{2,3,1,0:T(8,128)(2,1)S(1)} fusion(f32[8,2,128,128]{2,3,1,0:T(8,128)S(1)} %convert_element_type.139, f32[8,3,128,128]{2,3,1,0:T(8,128)S(1)} %convert_element_type.137, bf16[8,1,128,128]{2,3,1,0:T(8,128)(2,1)} %collective-permute-done.5, pred[]{:T(512)S(6)} %eq.39, pred[]{:T(512)S(6)} %eq.38, pred[]{:T(512)S(6)} %eq.37), kind=kLoop, calls=%fused_computation.46 | loop fusion | flops 1310720 | bytes 1572867 | tf_op jit(solution)/shard_map/convert
  92.4 0.9 copy.35
  93.5 0.9 copy.34
  (49 shorter events, 4.0 us)
Async XLA Ops:
  7.2 3.2 %copy-start = (bf16[128,1024]{1,0:T(8,128)(2,1)S(1)}, bf16[128,1024]{1,0:T(8,128)(2,1)}, u32[]{:S(2)}) copy-start(bf16[128,1024]{1,0:T(8,128)(2,1)} %param.9) | copy-start | bytes 786436
  7.2 7.1 %copy-start.9 = (bf16[128,1024]{1,0:T(8,128)(2,1)S(1)}, bf16[128,1024]{1,0:T(8,128)(2,1)}, u32[]{:S(2)}) copy-start(bf16[128,1024]{1,0:T(8,128)(2,1)} %param.13) | copy-start | bytes 786436
  7.2 26.0 %reduce-scatter.2.cloned.1.call-start = ((), (), s32[]{:S(2)}) async-start(), calls=%async_computation.1 | async-start | bytes 81920 | tf_op jit(solution)/shard_map/reduce_scatter | solution.py:33
  9.1 5.4 %copy-start.10 = (bf16[128,1024]{1,0:T(8,128)(2,1)S(1)}, bf16[128,1024]{1,0:T(8,128)(2,1)}, u32[]{:S(2)}) copy-start(bf16[128,1024]{1,0:T(8,128)(2,1)} %param.7) | copy-start | bytes 786436
  11.3 24.5 %collective-permute-start = (bf16[8,128,128]{2,1,0:T(8,128)(2,1)}, bf16[8,128,128]{2,1,0:T(8,128)(2,1)}, u32[]{:S(2)}, u32[]{:S(2)}) collective-permute-start(bf16[8,128,128]{2,1,0:T(8,128)(2,1)} %get-tuple-element.17), channel_id=1, source_target_pairs={{0,4},{4,0},{8,12},{12,8},{16,20},{20,16},{24,28},{28,24},{1,5},{5... | collective-permute-start | bytes 786440 | tf_op jit(solution)/shard_map/ppermute | solution.py:20
  14.5 1.4 %copy-start.1 = (bf16[128,1024]{1,0:T(8,128)(2,1)S(1)}, bf16[128,1024]{1,0:T(8,128)(2,1)}, u32[]{:S(2)}) copy-start(bf16[128,1024]{1,0:T(8,128)(2,1)} %param.8) | copy-start | bytes 786436
  14.6 2.3 %copy-start.3 = (bf16[16,8,8,128]{3,2,1,0:T(8,128)(2,1)}, bf16[16,8,8,128]{3,2,1,0:T(8,128)(2,1)S(1)}, u32[]{:S(2)}) copy-start(bf16[16,8,8,128]{3,2,1,0:T(8,128)(2,1)S(1)} %copy.74) | copy-start | bytes 786436
  14.6 18.6 %copy-start.11 = (s32[4]{0:T(128)S(1)}, s32[4]{0:T(128)}, u32[]{:S(2)}) copy-start(s32[4]{0:T(128)} %param.12) | copy-start | bytes 52
  33.2 5.3 %copy-start.4 = (bf16[16,8,8,128]{3,2,1,0:T(8,128)(2,1)S(1)}, bf16[16,8,8,128]{3,2,1,0:T(8,128)(2,1)}, u32[]{:S(2)}) copy-start(bf16[16,8,8,128]{3,2,1,0:T(8,128)(2,1)} %copy-done.3) | copy-start | bytes 786436
  36.9 7.6 %collective-permute-start.1 = (bf16[8,128,128]{2,1,0:T(8,128)(2,1)S(1)}, bf16[8,128,128]{2,1,0:T(8,128)(2,1)S(1)}, u32[]{:S(2)}, u32[]{:S(2)}) collective-permute-start(bf16[8,128,128]{2,1,0:T(8,128)(2,1)S(1)} %fusion.27), channel_id=1, source_target_pairs={{0,8},{8,0},{4,12},{12,4},{16,24},{24,16},{20,28},{28,20},{1,9},{9... | collective-permute-start | bytes 786440 | tf_op jit(solution)/shard_map/ppermute | solution.py:20
  38.9 9.3 %copy-start.2 = (bf16[8,128,128]{2,1,0:T(8,128)(2,1)S(1)}, bf16[8,128,128]{2,1,0:T(8,128)(2,1)}, u32[]{:S(2)}) copy-start(bf16[8,128,128]{2,1,0:T(8,128)(2,1)} %fusion.7) | copy-start | bytes 786436
  45.7 13.2 %collective-permute-start.2 = (bf16[8,128,128]{2,1,0:T(8,128)(2,1)S(1)}, bf16[8,128,128]{2,1,0:T(8,128)(2,1)S(1)}, u32[]{:S(2)}, u32[]{:S(2)}) collective-permute-start(bf16[8,128,128]{2,1,0:T(8,128)(2,1)S(1)} %get-tuple-element.15), channel_id=1, source_target_pairs={{0,16},{16,0},{4,20},{20,4},{8,24},{24,8},{12,28},{28,12},{1,17},{... | collective-permute-start | bytes 786440 | tf_op jit(solution)/shard_map/ppermute | solution.py:20
  49.3 17.6 %collective-permute-start.3 = (bf16[8,3,128,128]{2,3,1,0:T(8,128)(2,1)S(1)}, bf16[8,3,128,128]{2,3,1,0:T(8,128)(2,1)S(1)}, u32[]{:S(2)}, u32[]{:S(2)}) collective-permute-start(bf16[8,3,128,128]{2,3,1,0:T(8,128)(2,1)S(1)} %get-tuple-element.23), channel_id=1, source_target_pairs={{0,4},{4,0},{8,12},{12,8},{16,20},{20,16},{24,28},{28,24},{1,5},{5... | collective-permute-start | bytes 2359304 | tf_op jit(solution)/shard_map/ppermute | solution.py:20
  51.0 17.9 %copy-start.6 = (bf16[8,128,128]{2,1,0:T(8,128)(2,1)}, bf16[8,128,128]{2,1,0:T(8,128)(2,1)S(1)}, u32[]{:S(2)}) copy-start(bf16[8,128,128]{2,1,0:T(8,128)(2,1)S(1)} %fusion.8) | copy-start | bytes 786436
  67.2 11.1 %collective-permute-start.4 = (bf16[8,2,128,128]{2,3,1,0:T(8,128)(2,1)S(1)}, bf16[8,2,128,128]{2,3,1,0:T(8,128)(2,1)S(1)}, u32[]{:S(2)}, u32[]{:S(2)}) collective-permute-start(bf16[8,2,128,128]{2,3,1,0:T(8,128)(2,1)S(1)} %get-tuple-element.10), channel_id=1, source_target_pairs={{0,8},{8,0},{4,12},{12,4},{16,24},{24,16},{20,28},{28,20},{1,9},{9... | collective-permute-start | bytes 1572872 | tf_op jit(solution)/shard_map/ppermute | solution.py:20
  78.4 10.4 %copy-start.8 = (bf16[512,128]{1,0:T(8,128)(2,1)S(1)}, bf16[512,128]{1,0:T(8,128)(2,1)}, u32[]{:S(2)}) copy-start(bf16[512,128]{1,0:T(8,128)(2,1)} %param.11) | copy-start | bytes 393220
  79.2 11.4 %collective-permute-start.5 = (bf16[8,1,128,128]{2,3,1,0:T(8,128)(2,1)}, bf16[8,1,128,128]{2,3,1,0:T(8,128)(2,1)}, u32[]{:S(2)}, u32[]{:S(2)}) collective-permute-start(bf16[8,1,128,128]{2,3,1,0:T(8,128)(2,1)} %fusion.21), channel_id=1, source_target_pairs={{0,16},{16,0},{4,20},{20,4},{8,24},{24,8},{12,28},{28,12},{1,17},{... | collective-permute-start | bytes 786440 | tf_op jit(solution)/shard_map/ppermute | solution.py:20
  83.5 8.6 %copy-start.5 = (f32[8,128,128]{2,1,0:T(8,128)S(1)}, f32[8,128,128]{2,1,0:T(8,128)}, u32[]{:S(2)}) copy-start(f32[8,128,128]{2,1,0:T(8,128)} %fusion.41) | copy-start | bytes 1572868
  91.7 1.5 %copy-start.7 = (bf16[8,128,128]{2,1,0:T(8,128)(2,1)S(1)}, bf16[8,128,128]{2,1,0:T(8,128)(2,1)}, u32[]{:S(2)}) copy-start(bf16[8,128,128]{2,1,0:T(8,128)(2,1)} %copy-done.6) | copy-start | bytes 786436
Sparse Core Ops, SparseCore 0:
  11.0 22.1 reduce-scatter.1
where the time goes:
time: 102 us; the launch traced here: 101 us
  waiting for transfers between devices  45.1 us (44%)
  between operations  14.3 us (14%)
  matrix products  11.3 us (11%)
  starting transfers between devices  10.5 us (10%)
  local copies, waits for them, and re-layouts  8.06 us (8%)
  other arithmetic  6.46 us (6%)
  blocking collectives  5.31 us (5%)
    ppermute x6, waiting for transfers between devices, from_partner(): return lax.ppermute(block, axis, route)  28.8 us
    reduce_scatter x1, waiting for transfers between devices, local(): lax.psum_scatter(lax.dot_general(columns, hidden, (((0,), (1,)), ((), ())...  16.3 us
    ppermute x6, starting transfers between devices, from_partner(): return lax.ppermute(block, axis, route)  10.5 us
    unnamed x31, local copies, waits for them, and re-layouts  6.59 us
    all_gather x1, blocking collectives, local(): lax.all_gather(logit_grad, 'head', axis=0, tiled=True)  5.31 us
  transfers between devices with their start and end apart: 7, of which 6 were waited for; matrix products, arithmetic and copies ran while one was open for 17% of the time, Pallas kernels for 0%

commit v1 on v0

v1 whole, which is shorter than its diff:
```python
import functools

import jax
import jax.numpy as jnp
from jax import lax
from jax.experimental import pallas as pl
from jax.experimental.pallas import tpu as pltpu
from jax.sharding import PartitionSpec as P

DK = 128
MESH = pl.DeviceIdType.MESH
F32 = jnp.float32
BF16 = jnp.bfloat16
CHUNK_HEADS = 2


def dot(a, b, ca, cb):
    return lax.dot_general(a, b, (((ca,), (cb,)), ((), ())), preferred_element_type=F32)


def mix_kernel(
    seq_n, head_n,
    slot_ref, q_ref, k_ref, v_ref, hid_ref, gate_ref, g_ref,
    mixed_ref, gq_ref, gk_ref, gv_ref, ghid_ref,
    gatep, lp_send, lp_recv, lg_all,
    s_f32, s_bf, pair_recv, ls, h_send, r_send, r_recv, m_send, m_recv,
    intra, lev, lev1, gq_acc, gk_acc, gv_acc, wgt,
    lp_ss, lp_rs, lg_ss, lg_rs, pr_ss, pr_rs, up_ss, up_rs, dn_ss, dn_rs, m_ss, m_rs,
):
    tok = q_ref.shape[0]
    heads = q_ref.shape[1] // DK
    levels = lev.shape[0] + 2
    nb = levels - 2
    rows = heads * levels
    ch = min(CHUNK_HEADS, heads)
    chunks = heads // ch
    zn = seq_n // 2

    me = lax.axis_index("seq")
    hd = lax.axis_index("head")
    odd = me % 2
    z = me // 2
    pair = me + 1 - 2 * odd
    above = jnp.minimum(z + 1, zn - 1) * 2 + odd
    below = jnp.maximum(z - 1, 0) * 2 + odd
    is_top = z == zn - 1
    not_top = z < zn - 1
    not_low = z > 0
    bit = [(z // (1 << j)) % 2 for j in range(nb)]
    jstar = jnp.int32(nb)
    for j in reversed(range(nb)):
        jstar = jnp.where(bit[j] == 0, j, jstar)
    peers = [lax.rem(hd + d, head_n) for d in range(1, head_n)]

    barrier = pltpu.get_barrier_semaphore()
    pl.semaphore_signal(barrier, inc=1, device_id={"seq": pair}, device_id_type=MESH)
    for p in peers:
        pl.semaphore_signal(barrier, inc=1, device_id={"head": p}, device_id_type=MESH)

    @pl.when(not_top)
    def _():
        pl.semaphore_signal(barrier, inc=1, device_id={"seq": above}, device_id_type=MESH)

    @pl.when(not_low)
    def _():
        pl.semaphore_signal(barrier, inc=1, device_id={"seq": below}, device_id_type=MESH)

    def cs(k):
        return pl.ds(k * ch, ch)

    def copy(src, dst, ss, rs, where):
        return pltpu.make_async_remote_copy(
            src_ref=src, dst_ref=dst, send_sem=ss, recv_sem=rs, device_id=where, device_id_type=MESH
        )

    def lp_copy(d):
        return copy(
            lp_send.at[peers[d - 1]], lp_recv.at[d - 1], lp_ss.at[d - 1], lp_rs.at[d - 1],
            {"head": peers[d - 1]},
        )

    def lg_copy(d):
        return copy(
            lg_all.at[hd], lg_all.at[hd], lg_ss.at[d - 1], lg_rs.at[d - 1], {"head": peers[d - 1]}
        )

    def lg_wait(d):
        src = lax.rem(hd + head_n - d, head_n)
        copy(lg_all.at[src], lg_all.at[src], lg_ss.at[d - 1], lg_rs.at[d - 1], {"head": peers[d - 1]}).wait_recv()

    def pair_copy(k):
        return copy(s_bf.at[cs(k)], pair_recv.at[cs(k)], pr_ss.at[k], pr_rs.at[k], {"seq": pair})

    def up_copy(j, k):
        return copy(ls.at[j, cs(k)], ls.at[j, cs(k)], up_ss.at[j, k], up_rs.at[j, k], {"seq": above})

    def h_copy(k):
        j = jnp.minimum(jstar, nb - 1)
        return copy(h_send.at[cs(k)], ls.at[j, cs(k)], up_ss.at[j, k], up_rs.at[j, k], {"seq": above})

    def down_copy(j, k):
        return copy(r_send.at[j, cs(k)], r_recv.at[j, cs(k)], dn_ss.at[j, k], dn_rs.at[j, k], {"seq": below})

    def m_copy(k):
        return copy(m_send.at[cs(k)], m_recv.at[cs(k)], m_ss.at[k], m_rs.at[k], {"seq": pair})

    def hs(ref, h):
        return ref[:, h * DK:(h + 1) * DK]

    wide = head_n * rows
    r_from = lax.broadcasted_iota(jnp.int32, (wide, wide), 0)
    r_to = lax.broadcasted_iota(jnp.int32, (wide, wide), 1)
    in_dev = r_to % rows
    lev_of = in_dev // heads
    slot_of = jnp.zeros((wide, wide), jnp.int32)
    for l in range(levels):
        slot_of = jnp.where(lev_of == l, slot_ref[l], slot_of)
    target = (r_to // rows) * rows + (in_dev % heads) * levels + slot_of
    perm = jnp.where(r_from == target, 1.0, 0.0).astype(BF16)
    gatep[...] = dot(gate_ref[...], perm, 1, 0).astype(BF16)
    partial = dot(hid_ref[...], gatep[...], 1, 0).T
    for p in range(head_n):
        lp_send[p] = partial[p * rows:(p + 1) * rows, :]

    for h in range(ch):
        s = dot(hs(k_ref, h), hs(v_ref, h), 0, 0)
        s_f32[h] = s
        s_bf[h] = s.astype(BF16)

    for j in range(nb):
        @pl.when(bit[j] == 0)
        def _(j=j):
            ls[j] = jnp.zeros(ls.shape[1:], BF16)

    r_recv[nb] = jnp.zeros(r_recv.shape[1:], BF16)

    @pl.when(jnp.logical_and(is_top, odd == 0))
    def _():
        pair_recv[...] = jnp.zeros(pair_recv.shape, BF16)

    @pl.when(jnp.logical_and(is_top, odd == 1))
    def _():
        m_recv[...] = jnp.zeros(m_recv.shape, BF16)

    pl.semaphore_wait(
        barrier, head_n + jnp.where(not_top, 1, 0) + jnp.where(not_low, 1, 0)
    )
    for d in range(1, head_n):
        lp_copy(d).start()

    sends_s = jnp.logical_or(odd == 0, not_top)
    gets_s = jnp.logical_or(odd == 1, not_top)
    sends_m = jnp.logical_or(odd == 1, not_top)
    gets_m = jnp.logical_or(odd == 0, not_top)

    for k in range(chunks):
        if k > 0:
            for h in range(k * ch, (k + 1) * ch):
                s = dot(hs(k_ref, h), hs(v_ref, h), 0, 0)
                s_f32[h] = s
                s_bf[h] = s.astype(BF16)

        @pl.when(sends_s)
        def _(k=k):
            pair_copy(k).start()

    t_pos = lax.broadcasted_iota(jnp.int32, (tok, tok), 0)
    s_pos = lax.broadcasted_iota(jnp.int32, (tok, tok), 1)
    causal = jnp.where(t_pos >= s_pos, 1.0 / tok, 0.0)
    attend = {}
    for h in range(heads):
        a = (dot(hs(q_ref, h), hs(k_ref, h), 1, 1) * causal).astype(BF16)
        gv_acc[:, h * DK:(h + 1) * DK] = a.astype(F32)
        intra[:, h * DK:(h + 1) * DK] = dot(a, hs(v_ref, h), 1, 0)

    def f1(k):
        @pl.when(gets_s)
        def _():
            pair_copy(k).wait_recv()

        @pl.when(jnp.logical_and(not_top, jstar == 0))
        def _():
            h_send[cs(k)] = (s_f32[cs(k)] + pair_recv[cs(k)].astype(F32)).astype(BF16)
            h_copy(k).start()

    def f2(k):
        @pl.when(not_top)
        def _():
            for j in range(nb):
                @pl.when(bit[j] == 1)
                def _(j=j):
                    up_copy(j, k).wait_recv()

            @pl.when(jstar > 0)
            def _():
                total = s_f32[cs(k)] + pair_recv[cs(k)].astype(F32)
                for j in range(nb):
                    total = total + jnp.where(j < jstar, ls[j, cs(k)].astype(F32), 0.0)
                h_send[cs(k)] = total.astype(BF16)
                h_copy(k).start()

            for j in range(nb):
                @pl.when(jnp.logical_and(bit[j] == 1, j > jstar))
                def _(j=j):
                    up_copy(j, k).start()

    f1(0)

    mine = lp_send[hd]
    for d in range(1, head_n):
        lp_copy(d).wait_recv()
    for d in range(1, head_n):
        mine = mine + lp_recv[d - 1]
    soft = jnp.maximum(mine, 0.0) + jnp.log1p(jnp.exp(-jnp.abs(mine)))
    pad = jnp.zeros((DK - rows, tok), F32)
    soft_t = jnp.concatenate([soft, pad], 0).T if rows < DK else soft.T
    sig = jax.nn.sigmoid(mine)
    wgt[...] = soft_t

    def weight(l, h):
        return wgt[:, l * heads + h:l * heads + h + 1]

    def level_grads(k):
        for h in range(k * ch, (k + 1) * ch):
            gh = hs(g_ref, h).astype(F32)
            wgs = [(weight(l, h) * gh).astype(BF16) for l in range(1, levels)]
            grads = dot(hs(q_ref, h), jnp.concatenate(wgs, 1), 0, 0)
            lev1[h] = grads[:, :DK] * (1.0 / tok)
            for j in range(nb):
                lev[j, h] = grads[:, (j + 1) * DK:(j + 2) * DK] * (1.0 / (tok * 2 << j))

        @pl.when(is_top)
        def _():
            for j in reversed(range(nb)):
                r_send[j, cs(k)] = lev[j, cs(k)].astype(BF16)
                @pl.when(not_low)
                def _(j=j):
                    down_copy(j, k).start()

    def back(k):
        @pl.when(not_top)
        def _():
            for j in reversed(range(nb)):
                @pl.when(((z + 1) // (1 << j)) % 2 == 1)
                def _(j=j):
                    down_copy(j, k).wait_recv()

                @pl.when(bit[j] == 1)
                def _(j=j):
                    came = jnp.where(j < jstar, jstar, j)
                    r_send[j, cs(k)] = (lev[j, cs(k)] + r_recv[came, cs(k)].astype(F32)).astype(BF16)
                    down_copy(j, k).start()

        @pl.when(sends_m)
        def _():
            got = r_recv[jstar, cs(k)].astype(F32)
            own = jnp.where(odd == 1, 1.0, 0.0)
            m_send[cs(k)] = (got + own * lev1[cs(k)]).astype(BF16)
            m_copy(k).start()

    def span_grads(k):
        for h in range(k * ch, (k + 1) * ch):
            gh = hs(g_ref, h).astype(F32)
            w0 = (weight(0, h) * gh).astype(BF16)
            score = (dot(w0, hs(v_ref, h), 1, 1) * causal).astype(BF16)
            sl = slice(h * DK, (h + 1) * DK)
            a = gv_acc[:, sl].astype(BF16)
            gq_acc[:, sl] = dot(score, hs(k_ref, h), 1, 0)
            gk_acc[:, sl] = dot(score, hs(q_ref, h), 0, 0)
            gv_acc[:, sl] = dot(a, w0, 0, 0)

    for k in range(chunks):
        level_grads(k)
        if k + 1 < chunks:
            f1(k + 1)
        if k >= 1:
            f2(k - 1)
        if k >= 2:
            back(k - 2)
    f2(chunks - 1)
    for k in range(max(chunks - 2, 0), chunks):
        back(k)
        span_grads(k)
    for k in range(max(chunks - 2, 0)):
        span_grads(k)

    col = lax.broadcasted_iota(jnp.int32, (tok, DK), 1)
    scale1 = jnp.where(odd == 1, 1.0 / tok, 0.0)
    wg = jnp.zeros((tok, DK), F32)
    for k in range(chunks):
        @pl.when(is_top)
        def _(k=k):
            for j in range(nb):
                up_copy(j, k).wait_recv()

        for h in range(k * ch, (k + 1) * ch):
            sl = slice(h * DK, (h + 1) * DK)
            gh = hs(g_ref, h)
            gh32 = gh.astype(F32)
            part = intra[:, sl]
            out = weight(0, h) * part
            wg = jnp.where(col == h, jnp.sum(gh32 * part, 1, keepdims=True), wg)
            gq = gq_acc[:, sl]
            for l in range(1, levels):
                state = pair_recv[h] if l == 1 else ls[l - 2, h]
                scale = scale1 if l == 1 else 1.0 / (tok * (1 << (l - 1)))
                w = weight(l, h)
                lo = dot(hs(q_ref, h), state, 1, 0) * scale
                out = out + w * lo
                wg = jnp.where(col == l * heads + h, jnp.sum(gh32 * lo, 1, keepdims=True), wg)
                gq = gq + w * (dot(gh, state, 1, 1) * scale)
            mixed_ref[:, sl] = out.astype(BF16)
            gq_ref[:, sl] = gq.astype(BF16)

    lg_all[hd] = (wg.T[:rows, :] * sig).astype(BF16)
    for d in range(1, head_n):
        lg_copy(d).start()

    for k in range(chunks):
        @pl.when(gets_m)
        def _(k=k):
            m_copy(k).wait_recv()

        for h in range(k * ch, (k + 1) * ch):
            sl = slice(h * DK, (h + 1) * DK)
            sg = (r_recv[jstar, h].astype(F32) + m_recv[h].astype(F32)).astype(BF16)
            gk_ref[:, sl] = (gk_acc[:, sl] + dot(hs(v_ref, h), sg, 1, 1)).astype(BF16)
            gv_ref[:, sl] = (gv_acc[:, sl] + dot(hs(k_ref, h), sg, 1, 0)).astype(BF16)

    for d in range(1, head_n):
        lg_wait(d)
    every = jnp.concatenate([lg_all[p] for p in range(head_n)], 0)
    ghid_ref[...] = dot(every, gatep[...], 0, 1).astype(BF16)

    for d in range(1, head_n):
        lp_copy(d).wait_send()
        lg_copy(d).wait_send()
    for k in range(chunks):
        @pl.when(sends_s)
        def _(k=k):
            pair_copy(k).wait_send()

        @pl.when(sends_m)
        def _(k=k):
            m_copy(k).wait_send()

        for j in range(nb):
            @pl.when(jnp.logical_and(not_top, ((z + 1) // (1 << j)) % 2 == 1))
            def _(j=j, k=k):
                up_copy(j, k).wait_send()

            @pl.when(jnp.logical_and(not_low, bit[j] == 1))
            def _(j=j, k=k):
                down_copy(j, k).wait_send()


def local(seq_n, head_n, queries, keys, values, hidden, gate_weight, level_slot, out_grad):
    tok, width = queries.shape
    heads = width // DK
    levels = level_slot.shape[0]
    nb = levels - 2
    rows = heads * levels
    chunks = heads // min(CHUNK_HEADS, heads)
    feats = hidden.shape[1]
    wide = head_n * rows
    vm = pl.BlockSpec(memory_space=pltpu.VMEM)
    blk = (heads, DK, DK)
    sem = pltpu.SemaphoreType.DMA
    return pl.pallas_call(
        functools.partial(mix_kernel, seq_n, head_n),
        out_shape=[jax.ShapeDtypeStruct((tok, width), BF16)] * 4
        + [jax.ShapeDtypeStruct((tok, feats), BF16)],
        in_specs=[pl.BlockSpec(memory_space=pltpu.SMEM)] + [vm] * 6,
        out_specs=[vm] * 5,
        scratch_shapes=[
            pltpu.VMEM((feats, wide), BF16),
            pltpu.VMEM((head_n, rows, tok), F32),
            pltpu.VMEM((head_n - 1, rows, tok), F32),
            pltpu.VMEM((head_n, rows, tok), BF16),
            pltpu.VMEM(blk, F32),
            pltpu.VMEM(blk, BF16),
            pltpu.VMEM(blk, BF16),
            pltpu.VMEM((nb,) + blk, BF16),
            pltpu.VMEM(blk, BF16),
            pltpu.VMEM((nb,) + blk, BF16),
            pltpu.VMEM((nb + 1,) + blk, BF16),
            pltpu.VMEM(blk, BF16),
            pltpu.VMEM(blk, BF16),
            pltpu.VMEM((tok, width), F32),
            pltpu.VMEM((nb,) + blk, F32),
            pltpu.VMEM(blk, F32),
            pltpu.VMEM((tok, width), F32),
            pltpu.VMEM((tok, width), F32),
            pltpu.VMEM((tok, width), F32),
            pltpu.VMEM((tok, DK), F32),
            sem((head_n - 1,)), sem((head_n - 1,)),
            sem((head_n - 1,)), sem((head_n - 1,)),
            sem((chunks,)), sem((chunks,)),
            sem((nb, chunks)), sem((nb, chunks)),
            sem((nb, chunks)), sem((nb, chunks)),
            sem((chunks,)), sem((chunks,)),
        ],
        compiler_params=pltpu.CompilerParams(
            collective_id=0, has_side_effects=True, vmem_limit_bytes=48 << 20
        ),
    )(level_slot, queries, keys, values, hidden, gate_weight, out_grad)


def solution(mesh):
    both = P("seq", "head")
    return jax.shard_map(
        functools.partial(local, mesh.shape["seq"], mesh.shape["head"]),
        mesh=mesh,
        in_specs=(both, both, both, both, P("head", None), P(), both),
        out_specs=(both,) * 5,
        check_vma=False,
    )
```

time: 102 us -> 56.9 us (0.56)
  Pallas kernels: 0 us -> 46.2 us
  waiting for transfers between devices: 45.1 us -> 0 us
  between operations: 14.3 us -> 0.66 us
  matrix products: 11.3 us -> 0 us
  starting transfers between devices: 10.5 us -> 0 us
  other arithmetic: 6.46 us -> 0 us
  blocking collectives: 5.31 us -> 0 us
  local copies, waits for them, and re-layouts: 8.06 us -> 9.72 us
    pallas_call x0 -> x1, Pallas kernels: none -> 46.2 us  [local(): pl.pallas_call(functools.partial(mix_kernel, seq_n, head_n), out_shape=[j...]
    ppermute x6 -> x0, waiting for transfers between devices: 28.8 us -> none  [from_partner(): return lax.ppermute(block, axis, route)]
    reduce_scatter x1 -> x0, waiting for transfers between devices: 16.3 us -> none  [local(): lax.psum_scatter(lax.dot_general(columns, hidden, (((0,), (1,)), ((), ())...]
    dot_general x16 -> x0, matrix products: 11.3 us -> none  [the longest x1 1.87 us: local(): lax.dot_general(columns, hidden, (((0,), (1,)), ((), ())), preferred_elem...]
    ppermute x6 -> x0, starting transfers between devices: 10.5 us -> none  [from_partner(): return lax.ppermute(block, axis, route)]
    all_gather x1 -> x0, blocking collectives: 5.31 us -> none  [local(): lax.all_gather(logit_grad, 'head', axis=0, tiled=True)]
    convert_element_type x8 -> x0, other arithmetic: 3.94 us -> none  [the longest x1 1.67 us: local(): (weights[..., None] * grad_heads[:, :, None, :]).astype(jnp.bfloat16)]
    unnamed x31 -> x19, local copies, waits for them, and re-layouts: 6.59 us -> 9.72 us
  transfers between devices with their start and end apart: 7 -> 0, of which waited for: 6 -> 0; matrix products, arithmetic and copies ran while one was open for 17% -> 0% of each run, Pallas kernels for 0% -> 0%
where the time goes in v1:
time: 56.9 us; the launch traced here: 56.6 us
  Pallas kernels  46.2 us (81%)
  local copies, waits for them, and re-layouts  9.72 us (17%)
  between operations  0.66 us (1%)
    pallas_call x1, Pallas kernels, local(): pl.pallas_call(functools.partial(mix_kernel, seq_n, head_n), out_shape=[j...  46.2 us
    unnamed x19, local copies, waits for them, and re-layouts  9.72 us

profile of v1, /device:TPU:0, one launch (start us, length us, event | category | flops | bytes accessed | tf_op | source)
XLA Modules:
  0.0 56.6 jit_solution(10519251772108032639)
XLA Ops:
  0.6 0.0 copy-start
  0.6 0.9 %copy-done = bf16[128,1024]{1,0:T(8,128)(2,1)S(1)} copy-done((bf16[128,1024]{1,0:T(8,128)(2,1)S(1)}, bf16[128,1024]{1,0:T(8,128)(2,1)}, u32[]{:S(2)}) %copy-start) | copy-done | bytes 262168
  1.6 0.0 copy-start.1
  1.6 0.9 %copy-done.1 = bf16[128,1024]{1,0:T(8,128)(2,1)S(1)} copy-done((bf16[128,1024]{1,0:T(8,128)(2,1)S(1)}, bf16[128,1024]{1,0:T(8,128)(2,1)}, u32[]{:S(2)}) %copy-start.1) | copy-done | bytes 262168
  2.5 0.0 copy-start.2
  2.5 0.9 %copy-done.2 = bf16[128,1024]{1,0:T(8,128)(2,1)S(1)} copy-done((bf16[128,1024]{1,0:T(8,128)(2,1)S(1)}, bf16[128,1024]{1,0:T(8,128)(2,1)}, u32[]{:S(2)}) %copy-start.2) | copy-done | bytes 262168
  3.5 0.0 copy-start.3
  3.5 0.9 %copy-done.3 = bf16[128,1024]{1,0:T(8,128)(2,1)S(1)} copy-done((bf16[128,1024]{1,0:T(8,128)(2,1)S(1)}, bf16[128,1024]{1,0:T(8,128)(2,1)}, u32[]{:S(2)}) %copy-start.3) | copy-done | bytes 262168
  4.4 0.0 copy-start.4
  4.4 0.9 %copy-done.4 = bf16[128,512]{1,0:T(8,128)(2,1)S(1)} copy-done((bf16[128,512]{1,0:T(8,128)(2,1)S(1)}, bf16[128,512]{1,0:T(8,128)(2,1)}, u32[]{:S(2)}) %copy-start.4) | copy-done | bytes 131096
  5.3 0.0 copy-start.5
  5.3 0.9 %copy-done.5 = bf16[512,128]{1,0:T(8,128)(2,1)S(1)} copy-done((bf16[512,128]{1,0:T(8,128)(2,1)S(1)}, bf16[512,128]{1,0:T(8,128)(2,1)}, u32[]{:S(2)}) %copy-start.5) | copy-done | bytes 131096
  6.2 0.0 copy-start.6
  6.2 0.7 %copy-done.6 = s32[4]{0:T(128)S(1)} copy-done((s32[4]{0:T(128)S(1)}, s32[4]{0:T(128)}, u32[]{:S(2)}) %copy-start.6) | copy-done | bytes 40
  6.9 46.2 %shard_map.110 = (bf16[128,1024]{1,0:T(8,128)(2,1)S(1)}, bf16[128,1024]{1,0:T(8,128)(2,1)S(1)}, bf16[128,1024]{1,0:T(8,128)(2,1)S(1)}, bf16[128,1024]{1,0:T(8,128)(2,1)S(1)}, bf16[128,512]{1,0:T(8,128)(2,1)S(1)}) custom-call(s32[4]{0:T(128)S(1)} %copy-done.6, bf16[128,1024]{1,0:T(8,128)(2,1)S(1)} %copy-done, bf16[128,1024]{1,0:T(8,128)(2,1)S(1)} %copy-done.1, ...), custom_call_target="tpu_custom_call" | custom-call | tf_op jit(solution)/shard_map/pallas_call | solution.py:369
  53.2 0.7 %copy.17 = bf16[128,1024]{1,0:T(8,128)(2,1)} copy(bf16[128,1024]{1,0:T(8,128)(2,1)S(1)} %get-tuple-element.10) | data formatting | bytes 524288
  53.9 0.7 %copy.18 = bf16[128,1024]{1,0:T(8,128)(2,1)} copy(bf16[128,1024]{1,0:T(8,128)(2,1)S(1)} %get-tuple-element.11) | data formatting | bytes 524288
  54.6 0.7 %copy.19 = bf16[128,1024]{1,0:T(8,128)(2,1)} copy(bf16[128,1024]{1,0:T(8,128)(2,1)S(1)} %get-tuple-element.12) | data formatting | bytes 524288
  55.3 0.7 %copy.20 = bf16[128,1024]{1,0:T(8,128)(2,1)} copy(bf16[128,1024]{1,0:T(8,128)(2,1)S(1)} %get-tuple-element.13) | data formatting | bytes 524288
  56.0 0.7 %copy.21 = bf16[128,512]{1,0:T(8,128)(2,1)} copy(bf16[128,512]{1,0:T(8,128)(2,1)S(1)} %get-tuple-element.14) | data formatting | bytes 262144
Async XLA Ops:
  0.6 1.0 %copy-start = (bf16[128,1024]{1,0:T(8,128)(2,1)S(1)}, bf16[128,1024]{1,0:T(8,128)(2,1)}, u32[]{:S(2)}) copy-start(bf16[128,1024]{1,0:T(8,128)(2,1)} %q_ref.1) | copy-start | bytes 786436
  1.6 0.9 %copy-start.1 = (bf16[128,1024]{1,0:T(8,128)(2,1)S(1)}, bf16[128,1024]{1,0:T(8,128)(2,1)}, u32[]{:S(2)}) copy-start(bf16[128,1024]{1,0:T(8,128)(2,1)} %k_ref.1) | copy-start | bytes 786436
  2.5 0.9 %copy-start.2 = (bf16[128,1024]{1,0:T(8,128)(2,1)S(1)}, bf16[128,1024]{1,0:T(8,128)(2,1)}, u32[]{:S(2)}) copy-start(bf16[128,1024]{1,0:T(8,128)(2,1)} %v_ref.1) | copy-start | bytes 786436
  3.5 0.9 %copy-start.3 = (bf16[128,1024]{1,0:T(8,128)(2,1)S(1)}, bf16[128,1024]{1,0:T(8,128)(2,1)}, u32[]{:S(2)}) copy-start(bf16[128,1024]{1,0:T(8,128)(2,1)} %g_ref.1) | copy-start | bytes 786436
  4.4 0.9 %copy-start.4 = (bf16[128,512]{1,0:T(8,128)(2,1)S(1)}, bf16[128,512]{1,0:T(8,128)(2,1)}, u32[]{:S(2)}) copy-start(bf16[128,512]{1,0:T(8,128)(2,1)} %hid_ref.1) | copy-start | bytes 393220
  5.3 0.9 %copy-start.5 = (bf16[512,128]{1,0:T(8,128)(2,1)S(1)}, bf16[512,128]{1,0:T(8,128)(2,1)}, u32[]{:S(2)}) copy-start(bf16[512,128]{1,0:T(8,128)(2,1)} %gate_ref.1) | copy-start | bytes 393220
  6.2 0.7 %copy-start.6 = (s32[4]{0:T(128)S(1)}, s32[4]{0:T(128)}, u32[]{:S(2)}) copy-start(s32[4]{0:T(128)} %slot_ref.1) | copy-start | bytes 52

commit v2 on v1

--- a/solution.py
+++ b/solution.py
@@ -12,6 +12,7 @@
 F32 = jnp.float32
 BF16 = jnp.bfloat16
 CHUNK_HEADS = 2
+VMEM_ALL = (64 << 20) - (1 << 19)
 
 
 def dot(a, b, ca, cb):
@@ -20,11 +21,14 @@
 
 def mix_kernel(
     seq_n, head_n,
+    slot_hbm, q_hbm, k_hbm, v_hbm, hid_hbm, gate_hbm, g_hbm,
+    mixed_hbm, gq_hbm, gk_hbm, gv_hbm, ghid_hbm,
     slot_ref, q_ref, k_ref, v_ref, hid_ref, gate_ref, g_ref,
     mixed_ref, gq_ref, gk_ref, gv_ref, ghid_ref,
     gatep, lp_send, lp_recv, lg_all,
     s_f32, s_bf, pair_recv, ls, h_send, r_send, r_recv, m_send, m_recv,
-    intra, lev, lev1, gq_acc, gk_acc, gv_acc, wgt,
+    intra, lev, lev1, att_t, score, score_t, w_all, w0g, wlg,
+    in_sem, out_sem, hid_sem,
     lp_ss, lp_rs, lg_ss, lg_rs, pr_ss, pr_rs, up_ss, up_rs, dn_ss, dn_rs, m_ss, m_rs,
 ):
     tok = q_ref.shape[0]
@@ -36,6 +40,16 @@
     chunks = heads // ch
     zn = seq_n // 2
 
+    loads = [
+        pltpu.make_async_copy(src, dst, in_sem.at[i])
+        for i, (src, dst) in enumerate(
+            [(gate_hbm, gate_ref), (hid_hbm, hid_ref), (k_hbm, k_ref), (v_hbm, v_ref),
+             (q_hbm, q_ref), (g_hbm, g_ref), (slot_hbm, slot_ref)]
+        )
+    ]
+    for c in loads:
+        c.start()
+
     me = lax.axis_index("seq")
     hd = lax.axis_index("head")
     odd = me % 2
@@ -46,6 +60,8 @@
     is_top = z == zn - 1
     not_top = z < zn - 1
     not_low = z > 0
+    low_half = z < zn // 2
+    high_half = z >= zn // 2
     bit = [(z // (1 << j)) % 2 for j in range(nb)]
     jstar = jnp.int32(nb)
     for j in reversed(range(nb)):
@@ -68,6 +84,9 @@
     def cs(k):
         return pl.ds(k * ch, ch)
 
+    def group(k):
+        return range(k * ch, (k + 1) * ch)
+
     def copy(src, dst, ss, rs, where):
         return pltpu.make_async_remote_copy(
             src_ref=src, dst_ref=dst, send_sem=ss, recv_sem=rs, device_id=where, device_id_type=MESH
@@ -104,43 +123,41 @@
     def m_copy(k):
         return copy(m_send.at[cs(k)], m_recv.at[cs(k)], m_ss.at[k], m_rs.at[k], {"seq": pair})
 
+    def out_copy(i, src, dst, k):
+        sl = pl.ds(k * ch * DK, ch * DK)
+        return pltpu.make_async_copy(src.at[:, sl], dst.at[:, sl], out_sem.at[i, k])
+
     def hs(ref, h):
         return ref[:, h * DK:(h + 1) * DK]
 
     wide = head_n * rows
     r_from = lax.broadcasted_iota(jnp.int32, (wide, wide), 0)
-    r_to = lax.broadcasted_iota(jnp.int32, (wide, wide), 1)
+    r_to = lax.broadcasted_iota(jnp.int32, (1, wide), 1)
     in_dev = r_to % rows
+    loads[6].wait()
     lev_of = in_dev // heads
-    slot_of = jnp.zeros((wide, wide), jnp.int32)
+    slot_of = jnp.zeros((1, wide), jnp.int32)
     for l in range(levels):
         slot_of = jnp.where(lev_of == l, slot_ref[l], slot_of)
     target = (r_to // rows) * rows + (in_dev % heads) * levels + slot_of
     perm = jnp.where(r_from == target, 1.0, 0.0).astype(BF16)
+    loads[0].wait()
+    loads[1].wait()
     gatep[...] = dot(gate_ref[...], perm, 1, 0).astype(BF16)
     partial = dot(hid_ref[...], gatep[...], 1, 0).T
     for p in range(head_n):
         lp_send[p] = partial[p * rows:(p + 1) * rows, :]
 
-    for h in range(ch):
-        s = dot(hs(k_ref, h), hs(v_ref, h), 0, 0)
-        s_f32[h] = s
-        s_bf[h] = s.astype(BF16)
-
-    for j in range(nb):
-        @pl.when(bit[j] == 0)
-        def _(j=j):
-            ls[j] = jnp.zeros(ls.shape[1:], BF16)
-
-    r_recv[nb] = jnp.zeros(r_recv.shape[1:], BF16)
-
-    @pl.when(jnp.logical_and(is_top, odd == 0))
-    def _():
-        pair_recv[...] = jnp.zeros(pair_recv.shape, BF16)
-
-    @pl.when(jnp.logical_and(is_top, odd == 1))
-    def _():
-        m_recv[...] = jnp.zeros(m_recv.shape, BF16)
+    loads[2].wait()
+    loads[3].wait()
+
+    def states(hh):
+        for h in hh:
+            s = dot(hs(k_ref, h), hs(v_ref, h), 0, 0)
+            s_f32[h] = s
+            s_bf[h] = s.astype(BF16)
+
+    states(group(0))
 
     pl.semaphore_wait(
         barrier, head_n + jnp.where(not_top, 1, 0) + jnp.where(not_low, 1, 0)
@@ -153,25 +170,44 @@
     sends_m = jnp.logical_or(odd == 1, not_top)
     gets_m = jnp.logical_or(odd == 0, not_top)
 
-    for k in range(chunks):
-        if k > 0:
-            for h in range(k * ch, (k + 1) * ch):
-                s = dot(hs(k_ref, h), hs(v_ref, h), 0, 0)
-                s_f32[h] = s
-                s_bf[h] = s.astype(BF16)
-
+    def send_pair(k):
         @pl.when(sends_s)
-        def _(k=k):
+        def _():
             pair_copy(k).start()
+
+    send_pair(0)
+    states(range(ch, heads))
+    for k in range(1, chunks):
+        send_pair(k)
+
+    for j in range(nb):
+        @pl.when(bit[j] == 0)
+        def _(j=j):
+            ls[j] = jnp.zeros(ls.shape[1:], BF16)
+
+    r_recv[nb] = jnp.zeros(r_recv.shape[1:], BF16)
+
+    @pl.when(jnp.logical_and(is_top, odd == 0))
+    def _():
+        pair_recv[...] = jnp.zeros(pair_recv.shape, BF16)
+
+    @pl.when(jnp.logical_and(is_top, odd == 1))
+    def _():
+        m_recv[...] = jnp.zeros(m_recv.shape, BF16)
 
     t_pos = lax.broadcasted_iota(jnp.int32, (tok, tok), 0)
     s_pos = lax.broadcasted_iota(jnp.int32, (tok, tok), 1)
     causal = jnp.where(t_pos >= s_pos, 1.0 / tok, 0.0)
-    attend = {}
-    for h in range(heads):
-        a = (dot(hs(q_ref, h), hs(k_ref, h), 1, 1) * causal).astype(BF16)
-        gv_acc[:, h * DK:(h + 1) * DK] = a.astype(F32)
-        intra[:, h * DK:(h + 1) * DK] = dot(a, hs(v_ref, h), 1, 0)
+    causal_t = jnp.where(s_pos >= t_pos, 1.0 / tok, 0.0)
+
+    def inside(hh):
+        sc = [dot(hs(q_ref, h), hs(k_ref, h), 1, 1) for h in hh]
+        st = [dot(hs(k_ref, h), hs(q_ref, h), 1, 1) for h in hh]
+        at = [(s * causal).astype(BF16) for s in sc]
+        for h, s in zip(hh, st):
+            att_t[h] = (s * causal_t).astype(BF16)
+        for h, a in zip(hh, at):
+            intra[h] = dot(a, hs(v_ref, h), 1, 0)
 
     def f1(k):
         @pl.when(gets_s)
@@ -190,6 +226,11 @@
                 @pl.when(bit[j] == 1)
                 def _(j=j):
                     up_copy(j, k).wait_recv()
+
+            for j in range(nb):
+                @pl.when(jnp.logical_and(bit[j] == 1, j > jstar))
+                def _(j=j):
+                    up_copy(j, k).start()
 
             @pl.when(jstar > 0)
             def _():
@@ -199,12 +240,12 @@
                 h_send[cs(k)] = total.astype(BF16)
                 h_copy(k).start()
 
-            for j in range(nb):
-                @pl.when(jnp.logical_and(bit[j] == 1, j > jstar))
-                def _(j=j):
-                    up_copy(j, k).start()
-
+    loads[4].wait()
+    half = max(heads // 2, 1)
+    inside(range(half))
     f1(0)
+    inside(range(half, heads))
+    loads[5].wait()
 
     mine = lp_send[hd]
     for d in range(1, head_n):
@@ -215,16 +256,23 @@
     pad = jnp.zeros((DK - rows, tok), F32)
     soft_t = jnp.concatenate([soft, pad], 0).T if rows < DK else soft.T
     sig = jax.nn.sigmoid(mine)
-    wgt[...] = soft_t
-
-    def weight(l, h):
-        return wgt[:, l * heads + h:l * heads + h + 1]
+
+    def weigh(k):
+        for h in group(k):
+            gh = hs(g_ref, h).astype(F32)
+            for l in range(levels):
+                c = l * heads + h
+                w = jnp.broadcast_to(soft_t[:, c:c + 1], (tok, DK))
+                w_all[l, h] = w
+                if l == 0:
+                    w0g[h] = (w * gh).astype(BF16)
+                else:
+                    wlg[h, :, (l - 1) * DK:l * DK] = (w * gh).astype(BF16)
 
     def level_grads(k):
-        for h in range(k * ch, (k + 1) * ch):
-            gh = hs(g_ref, h).astype(F32)
-            wgs = [(weight(l, h) * gh).astype(BF16) for l in range(1, levels)]
-            grads = dot(hs(q_ref, h), jnp.concatenate(wgs, 1), 0, 0)
+        weigh(k)
+        for h in group(k):
+            grads = dot(hs(q_ref, h), wlg[h], 0, 0)
             lev1[h] = grads[:, :DK] * (1.0 / tok)
             for j in range(nb):
                 lev[j, h] = grads[:, (j + 1) * DK:(j + 2) * DK] * (1.0 / (tok * 2 << j))
@@ -259,33 +307,41 @@
             m_copy(k).start()
 
     def span_grads(k):
-        for h in range(k * ch, (k + 1) * ch):
-            gh = hs(g_ref, h).astype(F32)
-            w0 = (weight(0, h) * gh).astype(BF16)
-            score = (dot(w0, hs(v_ref, h), 1, 1) * causal).astype(BF16)
-            sl = slice(h * DK, (h + 1) * DK)
-            a = gv_acc[:, sl].astype(BF16)
-            gq_acc[:, sl] = dot(score, hs(k_ref, h), 1, 0)
-            gk_acc[:, sl] = dot(score, hs(q_ref, h), 0, 0)
-            gv_acc[:, sl] = dot(a, w0, 0, 0)
+        sc = [dot(w0g[h], hs(v_ref, h), 1, 1) for h in group(k)]
+        st = [dot(hs(v_ref, h), w0g[h], 1, 1) for h in group(k)]
+        for h, s, t in zip(group(k), sc, st):
+            score[h] = (s * causal).astype(BF16)
+            score_t[h] = (t * causal_t).astype(BF16)
+
+    def low(f, k):
+        @pl.when(low_half)
+        def _():
+            f(k)
+
+    def high(f, k):
+        @pl.when(high_half)
+        def _():
+            f(k)
 
     for k in range(chunks):
         level_grads(k)
         if k + 1 < chunks:
             f1(k + 1)
         if k >= 1:
-            f2(k - 1)
-        if k >= 2:
-            back(k - 2)
-    f2(chunks - 1)
-    for k in range(max(chunks - 2, 0), chunks):
-        back(k)
-        span_grads(k)
-    for k in range(max(chunks - 2, 0)):
-        span_grads(k)
+            low(f2, k - 1)
+    low(f2, chunks - 1)
+    for k in range(chunks):
+        high(back, k)
+        if k < chunks // 2:
+            span_grads(k)
+    for k in range(chunks):
+        low(back, k)
+        high(f2, k)
+        if k >= chunks // 2:
+            span_grads(k)
 
     col = lax.broadcasted_iota(jnp.int32, (tok, DK), 1)
-    scale1 = jnp.where(odd == 1, 1.0 / tok, 0.0)
+    scales = [jnp.where(odd == 1, 1.0 / tok, 0.0)] + [1.0 / (tok * 2 << j) for j in range(nb)]
     wg = jnp.zeros((tok, DK), F32)
     for k in range(chunks):
         @pl.when(is_top)
@@ -293,24 +349,27 @@
             for j in range(nb):
                 up_copy(j, k).wait_recv()
 
-        for h in range(k * ch, (k + 1) * ch):
+        cats = []
+        for h in group(k):
+            parts = [pair_recv[h]] + [ls[j, h] for j in range(nb)]
+            cats.append(jnp.concatenate(
+                [(p.astype(F32) * s).astype(BF16) for p, s in zip(parts, scales)], 1))
+        los = [dot(hs(q_ref, h), c, 1, 0) for h, c in zip(group(k), cats)]
+        gqs = [dot(score[h], hs(k_ref, h), 1, 0) + dot(wlg[h], c, 1, 1) for h, c in zip(group(k), cats)]
+        for h, lo, gq in zip(group(k), los, gqs):
             sl = slice(h * DK, (h + 1) * DK)
-            gh = hs(g_ref, h)
-            gh32 = gh.astype(F32)
-            part = intra[:, sl]
-            out = weight(0, h) * part
-            wg = jnp.where(col == h, jnp.sum(gh32 * part, 1, keepdims=True), wg)
-            gq = gq_acc[:, sl]
+            gh = hs(g_ref, h).astype(F32)
+            part = intra[h]
+            out = w_all[0, h] * part
+            wg = jnp.where(col == h, jnp.sum(gh * part, 1, keepdims=True), wg)
             for l in range(1, levels):
-                state = pair_recv[h] if l == 1 else ls[l - 2, h]
-                scale = scale1 if l == 1 else 1.0 / (tok * (1 << (l - 1)))
-                w = weight(l, h)
-                lo = dot(hs(q_ref, h), state, 1, 0) * scale
-                out = out + w * lo
-                wg = jnp.where(col == l * heads + h, jnp.sum(gh32 * lo, 1, keepdims=True), wg)
-                gq = gq + w * (dot(gh, state, 1, 1) * scale)
+                lol = lo[:, (l - 1) * DK:l * DK]
+                out = out + w_all[l, h] * lol
+                wg = jnp.where(col == l * heads + h, jnp.sum(gh * lol, 1, keepdims=True), wg)
             mixed_ref[:, sl] = out.astype(BF16)
             gq_ref[:, sl] = gq.astype(BF16)
+        out_copy(0, mixed_ref, mixed_hbm, k).start()
+        out_copy(1, gq_ref, gq_hbm, k).start()
 
     lg_all[hd] = (wg.T[:rows, :] * sig).astype(BF16)
     for d in range(1, head_n):
@@ -321,16 +380,22 @@
         def _(k=k):
             m_copy(k).wait_recv()
 
-        for h in range(k * ch, (k + 1) * ch):
+        sgs = [(r_recv[jstar, h].astype(F32) + m_recv[h].astype(F32)).astype(BF16) for h in group(k)]
+        gks = [dot(score_t[h], hs(q_ref, h), 1, 0) + dot(hs(v_ref, h), sg, 1, 1) for h, sg in zip(group(k), sgs)]
+        gvs = [dot(att_t[h], w0g[h], 1, 0) + dot(hs(k_ref, h), sg, 1, 0) for h, sg in zip(group(k), sgs)]
+        for h, gk, gv in zip(group(k), gks, gvs):
             sl = slice(h * DK, (h + 1) * DK)
-            sg = (r_recv[jstar, h].astype(F32) + m_recv[h].astype(F32)).astype(BF16)
-            gk_ref[:, sl] = (gk_acc[:, sl] + dot(hs(v_ref, h), sg, 1, 1)).astype(BF16)
-            gv_ref[:, sl] = (gv_acc[:, sl] + dot(hs(k_ref, h), sg, 1, 0)).astype(BF16)
+            gk_ref[:, sl] = gk.astype(BF16)
+            gv_ref[:, sl] = gv.astype(BF16)
+        out_copy(2, gk_ref, gk_hbm, k).start()
+        out_copy(3, gv_ref, gv_hbm, k).start()
 
     for d in range(1, head_n):
         lg_wait(d)
     every = jnp.concatenate([lg_all[p] for p in range(head_n)], 0)
     ghid_ref[...] = dot(every, gatep[...], 0, 1).astype(BF16)
+    last = pltpu.make_async_copy(ghid_ref, ghid_hbm, hid_sem)
+    last.start()
 
     for d in range(1, head_n):
         lp_copy(d).wait_send()
@@ -352,6 +417,21 @@
             @pl.when(jnp.logical_and(not_low, bit[j] == 1))
             def _(j=j, k=k):
                 down_copy(j, k).wait_send()
+        for i, (src, dst) in enumerate(
+            [(mixed_ref, mixed_hbm), (gq_ref, gq_hbm), (gk_ref, gk_hbm), (gv_ref, gv_hbm)]
+        ):
+            out_copy(i, src, dst, k).wait()
+    last.wait()
+
+
+def hand_over(*refs):
+    n = len(refs) // 2
+    sem = refs[-1]
+    copies = [pltpu.make_async_copy(refs[i], refs[n + i], sem.at[i]) for i in range(n)]
+    for c in copies:
+        c.start()
+    for c in copies:
+        c.wait()
 
 
 def local(seq_n, head_n, queries, keys, values, hidden, gate_weight, level_slot, out_grad):
@@ -363,16 +443,30 @@
     chunks = heads // min(CHUNK_HEADS, heads)
     feats = hidden.shape[1]
     wide = head_n * rows
-    vm = pl.BlockSpec(memory_space=pltpu.VMEM)
+    hbm = pl.BlockSpec(memory_space=pl.ANY)
     blk = (heads, DK, DK)
     sem = pltpu.SemaphoreType.DMA
-    return pl.pallas_call(
+    outs = [jax.ShapeDtypeStruct((tok, width), BF16)] * 4 + [
+        jax.ShapeDtypeStruct((tok, feats), BF16)
+    ]
+    made = pl.pallas_call(
         functools.partial(mix_kernel, seq_n, head_n),
-        out_shape=[jax.ShapeDtypeStruct((tok, width), BF16)] * 4
-        + [jax.ShapeDtypeStruct((tok, feats), BF16)],
-        in_specs=[pl.BlockSpec(memory_space=pltpu.SMEM)] + [vm] * 6,
-        out_specs=[vm] * 5,
+        out_shape=outs,
+        in_specs=[pl.BlockSpec(memory_space=pltpu.HBM)] * 7,
+        out_specs=[hbm] * 5,
         scratch_shapes=[
+            pltpu.SMEM((levels,), jnp.int32),
+            pltpu.VMEM((tok, width), BF16),
+            pltpu.VMEM((tok, width), BF16),
+            pltpu.VMEM((tok, width), BF16),
+            pltpu.VMEM((tok, feats), BF16),
+            pltpu.VMEM((feats, wide), BF16),
+            pltpu.VMEM((tok, width), BF16),
+            pltpu.VMEM((tok, width), BF16),
+            pltpu.VMEM((tok, width), BF16),
+            pltpu.VMEM((tok, width), BF16),
+            pltpu.VMEM((tok, width), BF16),
+            pltpu.VMEM((tok, feats), BF16),
             pltpu.VMEM((feats, wide), BF16),
             pltpu.VMEM((head_n, rows, tok), F32),
             pltpu.VMEM((head_n - 1, rows, tok), F32),
@@ -386,13 +480,16 @@
             pltpu.VMEM((nb + 1,) + blk, BF16),
             pltpu.VMEM(blk, BF16),
             pltpu.VMEM(blk, BF16),
-            pltpu.VMEM((tok, width), F32),
+            pltpu.VMEM(blk, F32),
             pltpu.VMEM((nb,) + blk, F32),
             pltpu.VMEM(blk, F32),
-            pltpu.VMEM((tok, width), F32),
-            pltpu.VMEM((tok, width), F32),
-            pltpu.VMEM((tok, width), F32),
-            pltpu.VMEM((tok, DK), F32),
+            pltpu.VMEM(blk, BF16),
+            pltpu.VMEM(blk, BF16),
+            pltpu.VMEM(blk, BF16),
+            pltpu.VMEM((levels,) + blk, F32),
+            pltpu.VMEM(blk, BF16),
+            pltpu.VMEM((heads, tok, (levels - 1) * DK), BF16),
+            sem((7,)), sem((4, chunks)), sem(()),
             sem((head_n - 1,)), sem((head_n - 1,)),
             sem((head_n - 1,)), sem((head_n - 1,)),
             sem((chunks,)), sem((chunks,)),
@@ -401,9 +498,17 @@
             sem((chunks,)), sem((chunks,)),
         ],
         compiler_params=pltpu.CompilerParams(
-            collective_id=0, has_side_effects=True, vmem_limit_bytes=48 << 20
+            collective_id=0, has_side_effects=True, vmem_limit_bytes=VMEM_ALL
         ),
     )(level_slot, queries, keys, values, hidden, gate_weight, out_grad)
+    return pl.pallas_call(
+        hand_over,
+        out_shape=outs,
+        in_specs=[hbm] * 5,
+        out_specs=[hbm] * 5,
+        scratch_shapes=[sem((5,))],
+        compiler_params=pltpu.CompilerParams(vmem_limit_bytes=VMEM_ALL),
+    )(*made)
 
 
 def solution(mesh):

time: 56.9 us -> 71.1 us (1.25)
  Pallas kernels: 46.2 us -> 70.3 us
  local copies, waits for them, and re-layouts: 9.72 us -> 0 us
    pallas_call x1 -> x2, Pallas kernels: 46.2 us -> 70.3 us  [the longest x1 36.9 us: local(): pl.pallas_call(hand_over, out_shape=outs, in_specs=[hbm] * 5, out_specs=[...]
    unnamed x19 -> x0, local copies, waits for them, and re-layouts: 9.72 us -> none
where the time goes in v2:
time: 71.1 us; the launch traced here: 70.9 us
  Pallas kernels  70.3 us (99%)
    pallas_call x1, Pallas kernels, local(): pl.pallas_call(hand_over, out_shape=outs, in_specs=[hbm] * 5, out_specs=[...  36.9 us
    pallas_call x1, Pallas kernels, local(): pl.pallas_call(functools.partial(mix_kernel, seq_n, head_n), out_shape=ou...  33.4 us

profile of v2, /device:TPU:0, one launch (start us, length us, event | category | flops | bytes accessed | tf_op | source)
XLA Modules:
  0.0 70.9 jit_solution(16731490943414026147)
XLA Ops:
  0.6 33.4 %shard_map.110 = (bf16[128,1024]{1,0:T(8,128)(2,1)}, bf16[128,1024]{1,0:T(8,128)(2,1)}, bf16[128,1024]{1,0:T(8,128)(2,1)}, bf16[128,1024]{1,0:T(8,128)(2,1)}, bf16[128,512]{1,0:T(8,128)(2,1)}) custom-call(s32[4]{0:T(128)} %slot_hbm.1, bf16[128,1024]{1,0:T(8,128)(2,1)} %q_hbm.1, bf16[128,1024]{1,0:T(8,128)(2,1)} %k_hbm.1, bf16[128,1024]{1,0:T(8,128)(2,1)} %v_hbm.1, ...), custom_call_target="tpu_custom_call" | custom-call | tf_op jit(solution)/shard_map/pallas_call | solution.py:452
  34.0 36.9 %shard_map.111 = (bf16[128,1024]{1,0:T(8,128)(2,1)}, bf16[128,1024]{1,0:T(8,128)(2,1)}, bf16[128,1024]{1,0:T(8,128)(2,1)}, bf16[128,1024]{1,0:T(8,128)(2,1)}, bf16[128,512]{1,0:T(8,128)(2,1)}) custom-call(bf16[128,1024]{1,0:T(8,128)(2,1)} %get-tuple-element.10.refs_0_, bf16[128,1024]{1,0:T(8,128)(2,1)} %get-tuple-element.11.refs_1_, ...), custom_call_target="tpu_custom_call" | custom-call | tf_op jit(solution)/shard_map/pallas_call | solution.py:504

commit v3 on v2

--- a/solution.py
+++ b/solution.py
@@ -243,8 +243,6 @@
     loads[4].wait()
     half = max(heads // 2, 1)
     inside(range(half))
-    f1(0)
-    inside(range(half, heads))
     loads[5].wait()
 
     mine = lp_send[hd]
@@ -281,15 +279,21 @@
         def _():
             for j in reversed(range(nb)):
                 r_send[j, cs(k)] = lev[j, cs(k)].astype(BF16)
-                @pl.when(not_low)
-                def _(j=j):
-                    down_copy(j, k).start()
-
-    def back(k):
+            top_send(nb - 1, k)
+
+    def top_send(j, k):
+        @pl.when(not_low)
+        def _():
+            down_copy(j, k).start()
+
+    def relay(k):
         @pl.when(not_top)
         def _():
             for j in reversed(range(nb)):
-                @pl.when(((z + 1) // (1 << j)) % 2 == 1)
+                needed = ((z + 1) // (1 << j)) % 2 == 1
+                if j == 0:
+                    needed = jnp.logical_and(needed, jstar > 0)
+                @pl.when(needed)
                 def _(j=j):
                     down_copy(j, k).wait_recv()
 
@@ -298,6 +302,11 @@
                     came = jnp.where(j < jstar, jstar, j)
                     r_send[j, cs(k)] = (lev[j, cs(k)] + r_recv[came, cs(k)].astype(F32)).astype(BF16)
                     down_copy(j, k).start()
+
+    def meet(k):
+        @pl.when(jstar == 0)
+        def _():
+            down_copy(0, k).wait_recv()
 
         @pl.when(sends_m)
         def _():
@@ -325,20 +334,25 @@
 
     for k in range(chunks):
         level_grads(k)
-        if k + 1 < chunks:
-            f1(k + 1)
+        f1(k)
         if k >= 1:
             low(f2, k - 1)
     low(f2, chunks - 1)
+
+    @pl.when(is_top)
+    def _():
+        for j in reversed(range(nb - 1)):
+            for k in range(chunks):
+                top_send(j, k)
+
+    rest = list(range(half, heads))
     for k in range(chunks):
-        high(back, k)
-        if k < chunks // 2:
-            span_grads(k)
-    for k in range(chunks):
-        low(back, k)
+        relay(k)
         high(f2, k)
-        if k >= chunks // 2:
-            span_grads(k)
+        span_grads(k)
+        part, rest = rest[:ch], rest[ch:]
+        if part:
+            inside(part)
 
     col = lax.broadcasted_iota(jnp.int32, (tok, DK), 1)
     scales = [jnp.where(odd == 1, 1.0 / tok, 0.0)] + [1.0 / (tok * 2 << j) for j in range(nb)]
@@ -370,6 +384,7 @@
             gq_ref[:, sl] = gq.astype(BF16)
         out_copy(0, mixed_ref, mixed_hbm, k).start()
         out_copy(1, gq_ref, gq_hbm, k).start()
+        meet(k)
 
     lg_all[hd] = (wg.T[:rows, :] * sig).astype(BF16)
     for d in range(1, head_n):
@@ -389,13 +404,13 @@
             gv_ref[:, sl] = gv.astype(BF16)
         out_copy(2, gk_ref, gk_hbm, k).start()
         out_copy(3, gv_ref, gv_hbm, k).start()
-
-    for d in range(1, head_n):
-        lg_wait(d)
-    every = jnp.concatenate([lg_all[p] for p in range(head_n)], 0)
-    ghid_ref[...] = dot(every, gatep[...], 0, 1).astype(BF16)
-    last = pltpu.make_async_copy(ghid_ref, ghid_hbm, hid_sem)
-    last.start()
+        if k == max(chunks // 2 - 1, 0):
+            for d in range(1, head_n):
+                lg_wait(d)
+            every = jnp.concatenate([lg_all[p] for p in range(head_n)], 0)
+            ghid_ref[...] = dot(every, gatep[...], 0, 1).astype(BF16)
+            last = pltpu.make_async_copy(ghid_ref, ghid_hbm, hid_sem)
+            last.start()
 
     for d in range(1, head_n):
         lp_copy(d).wait_send()
@@ -425,12 +440,16 @@
 
 
 def hand_over(*refs):
-    n = len(refs) // 2
+    n = len(refs) // 3
     sem = refs[-1]
-    copies = [pltpu.make_async_copy(refs[i], refs[n + i], sem.at[i]) for i in range(n)]
-    for c in copies:
+    ins = [pltpu.make_async_copy(refs[i], refs[2 * n + i], sem.at[0, i]) for i in range(n)]
+    outs = [pltpu.make_async_copy(refs[2 * n + i], refs[n + i], sem.at[1, i]) for i in range(n)]
+    for c in ins:
         c.start()
-    for c in copies:
+    for a, b in zip(ins, outs):
+        a.wait()
+        b.start()
+    for c in outs:
         c.wait()
 
 
@@ -506,7 +525,7 @@
         out_shape=outs,
         in_specs=[hbm] * 5,
         out_specs=[hbm] * 5,
-        scratch_shapes=[sem((5,))],
+        scratch_shapes=[pltpu.VMEM(o.shape, o.dtype) for o in outs] + [sem((2, 5))],
         compiler_params=pltpu.CompilerParams(vmem_limit_bytes=VMEM_ALL),
     )(*made)
 

time: 71.1 us -> 32.7 us (0.46)
  Pallas kernels: 70.3 us -> 31.9 us
    pallas_call x1, Pallas kernels: 36.9 us -> 2.04 us  [local(): pl.pallas_call(hand_over, out_shape=outs, in_specs=[hbm] * 5, out_specs=[...]
    pallas_call x1, Pallas kernels: 33.4 us -> 29.8 us  [local(): pl.pallas_call(functools.partial(mix_kernel, seq_n, head_n), out_shape=ou...]
where the time goes in v3:
time: 32.7 us; the launch traced here: 32.5 us
  Pallas kernels  31.9 us (98%)
  between operations  0.64 us (2%)
    pallas_call x1, Pallas kernels, local(): pl.pallas_call(functools.partial(mix_kernel, seq_n, head_n), out_shape=ou...  29.8 us
    pallas_call x1, Pallas kernels, local(): pl.pallas_call(hand_over, out_shape=outs, in_specs=[hbm] * 5, out_specs=[...  2.04 us

profile of v3, /device:TPU:0, one launch (start us, length us, event | category | flops | bytes accessed | tf_op | source)
XLA Modules:
  0.0 32.5 jit_solution(10760492442668142010)
XLA Ops:
  0.6 29.8 %shard_map.110 = (bf16[128,1024]{1,0:T(8,128)(2,1)}, bf16[128,1024]{1,0:T(8,128)(2,1)}, bf16[128,1024]{1,0:T(8,128)(2,1)}, bf16[128,1024]{1,0:T(8,128)(2,1)}, bf16[128,512]{1,0:T(8,128)(2,1)}) custom-call(s32[4]{0:T(128)} %slot_hbm.1, bf16[128,1024]{1,0:T(8,128)(2,1)} %q_hbm.1, bf16[128,1024]{1,0:T(8,128)(2,1)} %k_hbm.1, bf16[128,1024]{1,0:T(8,128)(2,1)} %v_hbm.1, ...), custom_call_target="tpu_custom_call" | custom-call | tf_op jit(solution)/shard_map/pallas_call | solution.py:471
  30.5 2.0 %shard_map.111 = (bf16[128,1024]{1,0:T(8,128)(2,1)}, bf16[128,1024]{1,0:T(8,128)(2,1)}, bf16[128,1024]{1,0:T(8,128)(2,1)}, bf16[128,1024]{1,0:T(8,128)(2,1)}, bf16[128,512]{1,0:T(8,128)(2,1)}) custom-call(bf16[128,1024]{1,0:T(8,128)(2,1)} %get-tuple-element.10.refs_0_, bf16[128,1024]{1,0:T(8,128)(2,1)} %get-tuple-element.11.refs_1_, ...), custom_call_target="tpu_custom_call" | custom-call | tf_op jit(solution)/shard_map/pallas_call | solution.py:523

commit v4 on v3

--- a/solution.py
+++ b/solution.py
@@ -12,7 +12,8 @@
 F32 = jnp.float32
 BF16 = jnp.bfloat16
 CHUNK_HEADS = 2
-VMEM_ALL = (64 << 20) - (1 << 19)
+SENT_HEADS = 1
+VMEM_ALL = (64 << 20) - (1 << 21)
 
 
 def dot(a, b, ca, cb):
@@ -22,13 +23,12 @@
 def mix_kernel(
     seq_n, head_n,
     slot_hbm, q_hbm, k_hbm, v_hbm, hid_hbm, gate_hbm, g_hbm,
-    mixed_hbm, gq_hbm, gk_hbm, gv_hbm, ghid_hbm,
+    mixed_ref, gq_ref, gk_ref, gv_ref, ghid_ref,
     slot_ref, q_ref, k_ref, v_ref, hid_ref, gate_ref, g_ref,
-    mixed_ref, gq_ref, gk_ref, gv_ref, ghid_ref,
     gatep, lp_send, lp_recv, lg_all,
     s_f32, s_bf, pair_recv, ls, h_send, r_send, r_recv, m_send, m_recv,
     intra, lev, lev1, att_t, score, score_t, w_all, w0g, wlg,
-    in_sem, out_sem, hid_sem,
+    in_sem,
     lp_ss, lp_rs, lg_ss, lg_rs, pr_ss, pr_rs, up_ss, up_rs, dn_ss, dn_rs, m_ss, m_rs,
 ):
     tok = q_ref.shape[0]
@@ -38,6 +38,8 @@
     rows = heads * levels
     ch = min(CHUNK_HEADS, heads)
     chunks = heads // ch
+    sent = min(SENT_HEADS, ch)
+    pieces = heads // sent
     zn = seq_n // 2
 
     loads = [
@@ -82,7 +84,10 @@
         pl.semaphore_signal(barrier, inc=1, device_id={"seq": below}, device_id_type=MESH)
 
     def cs(k):
-        return pl.ds(k * ch, ch)
+        return pl.ds(k * sent, sent)
+
+    def parts_of(k):
+        return range(k * ch // sent, (k + 1) * ch // sent)
 
     def group(k):
         return range(k * ch, (k + 1) * ch)
@@ -122,10 +127,6 @@
 
     def m_copy(k):
         return copy(m_send.at[cs(k)], m_recv.at[cs(k)], m_ss.at[k], m_rs.at[k], {"seq": pair})
-
-    def out_copy(i, src, dst, k):
-        sl = pl.ds(k * ch * DK, ch * DK)
-        return pltpu.make_async_copy(src.at[:, sl], dst.at[:, sl], out_sem.at[i, k])
 
     def hs(ref, h):
         return ref[:, h * DK:(h + 1) * DK]
@@ -175,10 +176,12 @@
         def _():
             pair_copy(k).start()
 
-    send_pair(0)
+    for c in parts_of(0):
+        send_pair(c)
     states(range(ch, heads))
     for k in range(1, chunks):
-        send_pair(k)
+        for c in parts_of(k):
+            send_pair(c)
 
     for j in range(nb):
         @pl.when(bit[j] == 0)
@@ -277,9 +280,10 @@
 
         @pl.when(is_top)
         def _():
-            for j in reversed(range(nb)):
-                r_send[j, cs(k)] = lev[j, cs(k)].astype(BF16)
-            top_send(nb - 1, k)
+            for c in parts_of(k):
+                for j in reversed(range(nb)):
+                    r_send[j, cs(c)] = lev[j, cs(c)].astype(BF16)
+                top_send(nb - 1, c)
 
     def top_send(j, k):
         @pl.when(not_low)
@@ -334,21 +338,25 @@
 
     for k in range(chunks):
         level_grads(k)
-        f1(k)
+        for c in parts_of(k):
+            f1(c)
         if k >= 1:
-            low(f2, k - 1)
-    low(f2, chunks - 1)
+            for c in parts_of(k - 1):
+                low(f2, c)
+    for c in parts_of(chunks - 1):
+        low(f2, c)
 
     @pl.when(is_top)
     def _():
         for j in reversed(range(nb - 1)):
-            for k in range(chunks):
-                top_send(j, k)
+            for c in range(pieces):
+                top_send(j, c)
 
     rest = list(range(half, heads))
     for k in range(chunks):
-        relay(k)
-        high(f2, k)
+        for c in parts_of(k):
+            relay(c)
+            high(f2, c)
         span_grads(k)
         part, rest = rest[:ch], rest[ch:]
         if part:
@@ -360,8 +368,9 @@
     for k in range(chunks):
         @pl.when(is_top)
         def _(k=k):
-            for j in range(nb):
-                up_copy(j, k).wait_recv()
+            for c in parts_of(k):
+                for j in range(nb):
+                    up_copy(j, c).wait_recv()
 
         cats = []
         for h in group(k):
@@ -382,9 +391,8 @@
                 wg = jnp.where(col == l * heads + h, jnp.sum(gh * lol, 1, keepdims=True), wg)
             mixed_ref[:, sl] = out.astype(BF16)
             gq_ref[:, sl] = gq.astype(BF16)
-        out_copy(0, mixed_ref, mixed_hbm, k).start()
-        out_copy(1, gq_ref, gq_hbm, k).start()
-        meet(k)
+        for c in parts_of(k):
+            meet(c)
 
     lg_all[hd] = (wg.T[:rows, :] * sig).astype(BF16)
     for d in range(1, head_n):
@@ -393,7 +401,8 @@
     for k in range(chunks):
         @pl.when(gets_m)
         def _(k=k):
-            m_copy(k).wait_recv()
+            for c in parts_of(k):
+                m_copy(c).wait_recv()
 
         sgs = [(r_recv[jstar, h].astype(F32) + m_recv[h].astype(F32)).astype(BF16) for h in group(k)]
         gks = [dot(score_t[h], hs(q_ref, h), 1, 0) + dot(hs(v_ref, h), sg, 1, 1) for h, sg in zip(group(k), sgs)]
@@ -402,20 +411,16 @@
             sl = slice(h * DK, (h + 1) * DK)
             gk_ref[:, sl] = gk.astype(BF16)
             gv_ref[:, sl] = gv.astype(BF16)
-        out_copy(2, gk_ref, gk_hbm, k).start()
-        out_copy(3, gv_ref, gv_hbm, k).start()
         if k == max(chunks // 2 - 1, 0):
             for d in range(1, head_n):
                 lg_wait(d)
             every = jnp.concatenate([lg_all[p] for p in range(head_n)], 0)
             ghid_ref[...] = dot(every, gatep[...], 0, 1).astype(BF16)
-            last = pltpu.make_async_copy(ghid_ref, ghid_hbm, hid_sem)
-            last.start()
 
     for d in range(1, head_n):
         lp_copy(d).wait_send()
         lg_copy(d).wait_send()
-    for k in range(chunks):
+    for k in range(pieces):
         @pl.when(sends_s)
         def _(k=k):
             pair_copy(k).wait_send()
@@ -432,24 +437,15 @@
             @pl.when(jnp.logical_and(not_low, bit[j] == 1))
             def _(j=j, k=k):
                 down_copy(j, k).wait_send()
-        for i, (src, dst) in enumerate(
-            [(mixed_ref, mixed_hbm), (gq_ref, gq_hbm), (gk_ref, gk_hbm), (gv_ref, gv_hbm)]
-        ):
-            out_copy(i, src, dst, k).wait()
-    last.wait()
 
 
 def hand_over(*refs):
-    n = len(refs) // 3
+    n = len(refs) // 2
     sem = refs[-1]
-    ins = [pltpu.make_async_copy(refs[i], refs[2 * n + i], sem.at[0, i]) for i in range(n)]
-    outs = [pltpu.make_async_copy(refs[2 * n + i], refs[n + i], sem.at[1, i]) for i in range(n)]
-    for c in ins:
+    copies = [pltpu.make_async_copy(refs[i], refs[n + i], sem.at[i]) for i in range(n)]
+    for c in copies:
         c.start()
-    for a, b in zip(ins, outs):
-        a.wait()
-        b.start()
-    for c in outs:
+    for c in copies:
         c.wait()
 
 
@@ -459,10 +455,11 @@
     levels = level_slot.shape[0]
     nb = levels - 2
     rows = heads * levels
-    chunks = heads // min(CHUNK_HEADS, heads)
+    chunks = heads // min(SENT_HEADS, CHUNK_HEADS, heads)
     feats = hidden.shape[1]
     wide = head_n * rows
     hbm = pl.BlockSpec(memory_space=pl.ANY)
+    vmem = pl.BlockSpec(memory_space=pltpu.VMEM)
     blk = (heads, DK, DK)
     sem = pltpu.SemaphoreType.DMA
     outs = [jax.ShapeDtypeStruct((tok, width), BF16)] * 4 + [
@@ -470,9 +467,9 @@
     ]
     made = pl.pallas_call(
         functools.partial(mix_kernel, seq_n, head_n),
-        out_shape=outs,
+        out_shape=[pltpu.VMEM(o.shape, o.dtype) for o in outs],
         in_specs=[pl.BlockSpec(memory_space=pltpu.HBM)] * 7,
-        out_specs=[hbm] * 5,
+        out_specs=[vmem] * 5,
         scratch_shapes=[
             pltpu.SMEM((levels,), jnp.int32),
             pltpu.VMEM((tok, width), BF16),
@@ -481,11 +478,6 @@
             pltpu.VMEM((tok, feats), BF16),
             pltpu.VMEM((feats, wide), BF16),
             pltpu.VMEM((tok, width), BF16),
-            pltpu.VMEM((tok, width), BF16),
-            pltpu.VMEM((tok, width), BF16),
-            pltpu.VMEM((tok, width), BF16),
-            pltpu.VMEM((tok, width), BF16),
-            pltpu.VMEM((tok, feats), BF16),
             pltpu.VMEM((feats, wide), BF16),
             pltpu.VMEM((head_n, rows, tok), F32),
             pltpu.VMEM((head_n - 1, rows, tok), F32),
@@ -508,7 +500,7 @@
             pltpu.VMEM((levels,) + blk, F32),
             pltpu.VMEM(blk, BF16),
             pltpu.VMEM((heads, tok, (levels - 1) * DK), BF16),
-            sem((7,)), sem((4, chunks)), sem(()),
+            sem((7,)),
             sem((head_n - 1,)), sem((head_n - 1,)),
             sem((head_n - 1,)), sem((head_n - 1,)),
             sem((chunks,)), sem((chunks,)),
@@ -523,10 +515,9 @@
     return pl.pallas_call(
         hand_over,
         out_shape=outs,
-        in_specs=[hbm] * 5,
+        in_specs=[vmem] * 5,
         out_specs=[hbm] * 5,
-        scratch_shapes=[pltpu.VMEM(o.shape, o.dtype) for o in outs] + [sem((2, 5))],
-        compiler_params=pltpu.CompilerParams(vmem_limit_bytes=VMEM_ALL),
+        scratch_shapes=[sem((5,))],
     )(*made)
 
 

time: 32.7 us -> 34.3 us (1.049)
  local copies, waits for them, and re-layouts: 0 us -> 3.42 us
  Pallas kernels: 31.9 us -> 30.1 us
    unnamed x0 -> x10, local copies, waits for them, and re-layouts: none -> 3.42 us
    pallas_call x2, Pallas kernels: 31.9 us -> 30.1 us  [the longest x1 27.8 us: local(): pl.pallas_call(functools.partial(mix_kernel, seq_n, head_n), out_shape=[p...]
where the time goes in v4:
time: 34.3 us; the launch traced here: 34.1 us
  Pallas kernels  30.1 us (88%)
  local copies, waits for them, and re-layouts  3.42 us (10%)
  between operations  0.65 us (2%)
    pallas_call x1, Pallas kernels, local(): pl.pallas_call(functools.partial(mix_kernel, seq_n, head_n), out_shape=[p...  27.8 us
    unnamed x10, local copies, waits for them, and re-layouts  3.42 us
    pallas_call x1, Pallas kernels, local(): pl.pallas_call(hand_over, out_shape=outs, in_specs=[vmem] * 5, out_specs=...  2.26 us

profile of v4, /device:TPU:0, one launch (start us, length us, event | category | flops | bytes accessed | tf_op | source)
XLA Modules:
  0.0 34.1 jit_solution(370757111142821061)
XLA Ops:
  0.6 27.8 %shard_map.110 = (bf16[128,1024]{1,0:T(8,128)(2,1)S(1)}, bf16[128,1024]{1,0:T(8,128)(2,1)S(1)}, bf16[128,1024]{1,0:T(8,128)(2,1)S(1)}, bf16[128,1024]{1,0:T(8,128)(2,1)S(1)}, bf16[128,512]{1,0:T(8,128)(2,1)S(1)}) custom-call(s32[4]{0:T(128)} %slot_hbm.1, bf16[128,1024]{1,0:T(8,128)(2,1)} %q_hbm.1, bf16[128,1024]{1,0:T(8,128)(2,1)} %k_hbm.1, ...), custom_call_target="tpu_custom_call" | custom-call | tf_op jit(solution)/shard_map/pallas_call | solution.py:468
  28.4 0.0 copy-start
  28.4 0.7 %copy-done = bf16[128,1024]{1,0:T(8,128)(2,1)} copy-done((bf16[128,1024]{1,0:T(8,128)(2,1)}, bf16[128,1024]{1,0:T(8,128)(2,1)S(1)}, u32[]{:S(2)}) %copy-start) | copy-done | bytes 262168
  29.1 0.0 copy-start.1
  29.1 0.7 %copy-done.1 = bf16[128,1024]{1,0:T(8,128)(2,1)} copy-done((bf16[128,1024]{1,0:T(8,128)(2,1)}, bf16[128,1024]{1,0:T(8,128)(2,1)S(1)}, u32[]{:S(2)}) %copy-start.1) | copy-done | bytes 262168
  29.8 0.0 copy-start.2
  29.8 0.7 %copy-done.2 = bf16[128,1024]{1,0:T(8,128)(2,1)} copy-done((bf16[128,1024]{1,0:T(8,128)(2,1)}, bf16[128,1024]{1,0:T(8,128)(2,1)S(1)}, u32[]{:S(2)}) %copy-start.2) | copy-done | bytes 262168
  30.5 0.0 copy-start.3
  30.5 0.7 %copy-done.3 = bf16[128,1024]{1,0:T(8,128)(2,1)} copy-done((bf16[128,1024]{1,0:T(8,128)(2,1)}, bf16[128,1024]{1,0:T(8,128)(2,1)S(1)}, u32[]{:S(2)}) %copy-start.3) | copy-done | bytes 262168
  31.2 0.0 copy-start.4
  31.2 0.6 %copy-done.4 = bf16[128,512]{1,0:T(8,128)(2,1)} copy-done((bf16[128,512]{1,0:T(8,128)(2,1)}, bf16[128,512]{1,0:T(8,128)(2,1)S(1)}, u32[]{:S(2)}) %copy-start.4) | copy-done | bytes 131096
  31.9 2.3 %shard_map.111 = (bf16[128,1024]{1,0:T(8,128)(2,1)}, bf16[128,1024]{1,0:T(8,128)(2,1)}, bf16[128,1024]{1,0:T(8,128)(2,1)}, bf16[128,1024]{1,0:T(8,128)(2,1)}, bf16[128,512]{1,0:T(8,128)(2,1)}) custom-call(bf16[128,1024]{1,0:T(8,128)(2,1)} %copy-done, bf16[128,1024]{1,0:T(8,128)(2,1)} %copy-done.1, bf16[128,1024]{1,0:T(8,128)(2,1)} %copy-done.2, ...), custom_call_target="tpu_custom_call" | custom-call | tf_op jit(solution)/shard_map/pallas_call | solution.py:515
Async XLA Ops:
  28.4 0.7 %copy-start = (bf16[128,1024]{1,0:T(8,128)(2,1)}, bf16[128,1024]{1,0:T(8,128)(2,1)S(1)}, u32[]{:S(2)}) copy-start(bf16[128,1024]{1,0:T(8,128)(2,1)S(1)} %get-tuple-element.10.refs_0_) | copy-start | bytes 786436
  29.1 0.7 %copy-start.1 = (bf16[128,1024]{1,0:T(8,128)(2,1)}, bf16[128,1024]{1,0:T(8,128)(2,1)S(1)}, u32[]{:S(2)}) copy-start(bf16[128,1024]{1,0:T(8,128)(2,1)S(1)} %get-tuple-element.11.refs_1_) | copy-start | bytes 786436
  29.8 0.7 %copy-start.2 = (bf16[128,1024]{1,0:T(8,128)(2,1)}, bf16[128,1024]{1,0:T(8,128)(2,1)S(1)}, u32[]{:S(2)}) copy-start(bf16[128,1024]{1,0:T(8,128)(2,1)S(1)} %get-tuple-element.12.refs_2_) | copy-start | bytes 786436
  30.5 0.7 %copy-start.3 = (bf16[128,1024]{1,0:T(8,128)(2,1)}, bf16[128,1024]{1,0:T(8,128)(2,1)S(1)}, u32[]{:S(2)}) copy-start(bf16[128,1024]{1,0:T(8,128)(2,1)S(1)} %get-tuple-element.13.refs_3_) | copy-start | bytes 786436
  31.2 0.6 %copy-start.4 = (bf16[128,512]{1,0:T(8,128)(2,1)}, bf16[128,512]{1,0:T(8,128)(2,1)S(1)}, u32[]{:S(2)}) copy-start(bf16[128,512]{1,0:T(8,128)(2,1)S(1)} %get-tuple-element.14.refs_4_) | copy-start | bytes 393220

commit v5 on v4

--- a/solution.py
+++ b/solution.py
@@ -49,7 +49,7 @@
              (q_hbm, q_ref), (g_hbm, g_ref), (slot_hbm, slot_ref)]
         )
     ]
-    for c in loads:
+    for c in loads[6:] + loads[:6]:
         c.start()
 
     me = lax.axis_index("seq")
@@ -515,9 +515,10 @@
     return pl.pallas_call(
         hand_over,
         out_shape=outs,
-        in_specs=[vmem] * 5,
+        in_specs=[hbm] * 5,
         out_specs=[hbm] * 5,
         scratch_shapes=[sem((5,))],
+        compiler_params=pltpu.CompilerParams(vmem_limit_bytes=4 << 20),
     )(*made)
 
 

time: 34.3 us -> 29.7 us (0.87)
  local copies, waits for them, and re-layouts: 3.42 us -> 0 us
  Pallas kernels: 30.1 us -> 28.9 us
    unnamed x10 -> x0, local copies, waits for them, and re-layouts: 3.42 us -> none
    pallas_call x1, Pallas kernels: 2.26 us -> 1.05 us  [local(): pl.pallas_call(hand_over, out_shape=outs, in_specs=[hbm] * 5, out_specs=[...]
where the time goes in v5:
time: 29.7 us; the launch traced here: 29.5 us
  Pallas kernels  28.9 us (97%)
  between operations  0.64 us (2%)
    pallas_call x1, Pallas kernels, local(): pl.pallas_call(functools.partial(mix_kernel, seq_n, head_n), out_shape=[p...  27.8 us
    pallas_call x1, Pallas kernels, local(): pl.pallas_call(hand_over, out_shape=outs, in_specs=[hbm] * 5, out_specs=[...  1.05 us

profile of v5, /device:TPU:0, one launch (start us, length us, event | category | flops | bytes accessed | tf_op | source)
XLA Modules:
  0.0 29.5 jit_solution(6185362782488607029)
XLA Ops:
  0.6 27.8 %shard_map.110 = (bf16[128,1024]{1,0:T(8,128)(2,1)S(1)}, bf16[128,1024]{1,0:T(8,128)(2,1)S(1)}, bf16[128,1024]{1,0:T(8,128)(2,1)S(1)}, bf16[128,1024]{1,0:T(8,128)(2,1)S(1)}, bf16[128,512]{1,0:T(8,128)(2,1)S(1)}) custom-call(s32[4]{0:T(128)} %slot_hbm.1, bf16[128,1024]{1,0:T(8,128)(2,1)} %q_hbm.1, bf16[128,1024]{1,0:T(8,128)(2,1)} %k_hbm.1, ...), custom_call_target="tpu_custom_call" | custom-call | tf_op jit(solution)/shard_map/pallas_call | solution.py:468
  28.5 1.0 %shard_map.111 = (bf16[128,1024]{1,0:T(8,128)(2,1)}, bf16[128,1024]{1,0:T(8,128)(2,1)}, bf16[128,1024]{1,0:T(8,128)(2,1)}, bf16[128,1024]{1,0:T(8,128)(2,1)}, bf16[128,512]{1,0:T(8,128)(2,1)}) custom-call(bf16[128,1024]{1,0:T(8,128)(2,1)S(1)} %get-tuple-element.10.refs_0_, bf16[128,1024]{1,0:T(8,128)(2,1)S(1)} %get-tuple-element.11.refs_1_, ...), custom_call_target="tpu_custom_call" | custom-call | tf_op jit(solution)/shard_map/pallas_call | solution.py:515

commit v6 on v5

--- a/solution.py
+++ b/solution.py
@@ -11,7 +11,7 @@
 MESH = pl.DeviceIdType.MESH
 F32 = jnp.float32
 BF16 = jnp.bfloat16
-CHUNK_HEADS = 2
+CHUNK_HEADS = 4
 SENT_HEADS = 1
 VMEM_ALL = (64 << 20) - (1 << 21)
 

time: 29.7 us -> 31 us (1.044)
  Pallas kernels: 28.9 us -> 30.2 us
    pallas_call x1, Pallas kernels: 27.8 us -> 29.1 us  [local(): pl.pallas_call(functools.partial(mix_kernel, seq_n, head_n), out_shape=[p...]
where the time goes in v6:
time: 31 us; the launch traced here: 30.8 us
  Pallas kernels  30.2 us (97%)
  between operations  0.64 us (2%)
    pallas_call x1, Pallas kernels, local(): pl.pallas_call(functools.partial(mix_kernel, seq_n, head_n), out_shape=[p...  29.1 us
    pallas_call x1, Pallas kernels, local(): pl.pallas_call(hand_over, out_shape=outs, in_specs=[hbm] * 5, out_specs=[...  1.05 us

profile of v6, /device:TPU:0, one launch (start us, length us, event | category | flops | bytes accessed | tf_op | source)
XLA Modules:
  0.0 30.8 jit_solution(1556647035431303068)
XLA Ops:
  0.6 29.1 %shard_map.110 = (bf16[128,1024]{1,0:T(8,128)(2,1)S(1)}, bf16[128,1024]{1,0:T(8,128)(2,1)S(1)}, bf16[128,1024]{1,0:T(8,128)(2,1)S(1)}, bf16[128,1024]{1,0:T(8,128)(2,1)S(1)}, bf16[128,512]{1,0:T(8,128)(2,1)S(1)}) custom-call(s32[4]{0:T(128)} %slot_hbm.1, bf16[128,1024]{1,0:T(8,128)(2,1)} %q_hbm.1, bf16[128,1024]{1,0:T(8,128)(2,1)} %k_hbm.1, ...), custom_call_target="tpu_custom_call" | custom-call | tf_op jit(solution)/shard_map/pallas_call | solution.py:468
  29.8 1.0 %shard_map.111 = (bf16[128,1024]{1,0:T(8,128)(2,1)}, bf16[128,1024]{1,0:T(8,128)(2,1)}, bf16[128,1024]{1,0:T(8,128)(2,1)}, bf16[128,1024]{1,0:T(8,128)(2,1)}, bf16[128,512]{1,0:T(8,128)(2,1)}) custom-call(bf16[128,1024]{1,0:T(8,128)(2,1)S(1)} %get-tuple-element.10.refs_0_, bf16[128,1024]{1,0:T(8,128)(2,1)S(1)} %get-tuple-element.11.refs_1_, ...), custom_call_target="tpu_custom_call" | custom-call | tf_op jit(solution)/shard_map/pallas_call | solution.py:515
